TPU v7x, 128 devices: a whole 4x4x4 slice. The times are simulated.
128 devices in a mesh: rows: 16 (over y_hi, x, core), chan: 8 (over z, y_lo).
Axes of the slice: x: 4, y: 4 (y_hi: 2, y_lo: 2; y = y_hi * 2 + y_lo), z: 4, core: 2. Of those that a mesh axis runs over, the one named last changes fastest.
Arguments:
- activation: bfloat16 [1, 128, 128, 2048], P(None, 'chan', 'rows'), may hold values from -6 to 6
- out_grad: bfloat16 [1, 128, 128, 2048], P(None, 'chan', 'rows'), may hold values from -6 to 6
- weights: bfloat16 [9, 128, 128], replicated, may hold values from -0.1875 to 0.1875
- biases: float32 [128], replicated, may hold values from -3 to 3
Outputs:
- input_grad: bfloat16 [1, 128, 128, 2048], P(None, 'chan', 'rows')
- weight_grad: float32 [9, 128, 128], P(None, 'chan')
- bias_grad: float32 [128], P('chan')
All inputs are finite; a program needn't handle non-finite values.
Results may differ from a plain program's by a relative error of at most 0.0075.
Values may be sent and summed in bfloat16 or wider, within the bound.
A program may use at most 64 MiB of HBM per device.

v0:
```python
import jax
import jax.numpy as jnp
from jax import lax
from jax.sharding import PartitionSpec as P


def extended(block, sides, width):
    for axis, dim in sides:
        count = lax.axis_size(axis)
        forward = [(i, i + 1) for i in range(count - 1)]
        backward = [(target, source) for source, target in forward]
        low = lax.ppermute(
            lax.slice_in_dim(block, block.shape[dim] - width, None, axis=dim), axis, forward
        )
        high = lax.ppermute(lax.slice_in_dim(block, 0, width, axis=dim), axis, backward)
        block = jnp.concatenate([low, block, high], axis=dim)
    return block


def forward_taps(kernel, padded, height, extent):
    total = None
    for tap_row in range(3):
        for tap_col in range(3):
            window = padded[
                :, :, 4 * tap_row : 4 * tap_row + height, 4 * tap_col : 4 * tap_col + extent
            ]
            term = jnp.einsum(
                "oi,bihw->bohw",
                kernel[3 * tap_row + tap_col],
                window,
                preferred_element_type=jnp.float32,
            )
            total = term if total is None else total + term
    return total


def backward_taps(kernel, delta_pad, height, extent):
    total = None
    for tap_row in range(3):
        for tap_col in range(3):
            back = delta_pad[
                :,
                :,
                8 - 4 * tap_row : 8 - 4 * tap_row + height,
                8 - 4 * tap_col : 8 - 4 * tap_col + extent,
            ]
            term = jnp.einsum(
                "oi,bohw->bihw",
                kernel[3 * tap_row + tap_col],
                back,
                preferred_element_type=jnp.float32,
            )
            total = term if total is None else total + term
    return total


def kernel_taps(delta, padded, height, extent):
    grads = []
    for tap_row in range(3):
        for tap_col in range(3):
            window = padded[
                :, :, 4 * tap_row : 4 * tap_row + height, 4 * tap_col : 4 * tap_col + extent
            ]
            grads.append(
                jnp.einsum("bohw,bihw->oi", delta, window, preferred_element_type=jnp.float32)
            )
    return jnp.stack(grads, axis=0)


def local_delta(pre, out_grad):
    sig = jax.nn.sigmoid(pre)
    return (out_grad.astype(jnp.float32) * sig * (1.0 + pre * (1.0 - sig))).astype(jnp.bfloat16)


def shards(activation, out_grad, weights, biases):
    tile_ch = activation.shape[1]
    height = activation.shape[2]
    extent = activation.shape[3]
    offset = lax.axis_index("chan") * tile_ch
    w_out = lax.dynamic_slice_in_dim(weights, offset, tile_ch, 1)
    w_in = lax.dynamic_slice_in_dim(weights, offset, tile_ch, 2)
    bias_own = lax.dynamic_slice_in_dim(biases, offset, tile_ch, 0)
    act_rim = extended(activation, (("rows", 2),), 4)
    act_all = lax.all_gather(act_rim, "chan", axis=1, tiled=True)
    act_pad = jnp.pad(act_all, ((0, 0), (0, 0), (0, 0), (4, 4)))
    pre = forward_taps(w_out, act_pad, height, extent) + bias_own[None, :, None, None]
    delta = local_delta(pre, out_grad)
    delta_rim = extended(delta, (("rows", 2),), 4)
    delta_all = lax.all_gather(delta_rim, "chan", axis=1, tiled=True)
    delta_pad = jnp.pad(delta_all, ((0, 0), (0, 0), (0, 0), (4, 4)))
    grad_in = backward_taps(w_in, delta_pad, height, extent).astype(jnp.bfloat16)
    kern_part = kernel_taps(delta, act_pad, height, extent)
    bias_part = jnp.sum(delta.astype(jnp.float32), axis=(0, 2, 3))
    weight_grad, bias_grad = lax.psum((kern_part, bias_part), "rows")
    return (grad_in, weight_grad, bias_grad)


def solution(mesh):
    return jax.shard_map(
        shards,
        mesh=mesh,
        in_specs=(P(None, "chan", "rows", None), P(None, "chan", "rows", None), P(), P()),
        out_specs=(P(None, "chan", "rows", None), P(None, "chan", None), P("chan")),
        check_vma=False,
    )
```

profile of v0, /device:TPU:1, one launch (start us, length us, event | category | flops | bytes accessed | tf_op | source)
XLA Modules:
  0.0 533.4 jit_solution(16826318230618954761)
XLA Ops:
  8.6 4.5 collective-permute-start
  13.2 1.9 collective-permute-start.1
  16.5 4.4 collective-permute-done.1
  22.8 172.1 %all-gather.3.cloned.1.call-done = bf16[1,128,16,2048]{3,1,2,0:T(8,128)(2,1)} async-done(((bf16[1,16,16,2048]{3,1,2,0:T(8,128)(2,1)}), bf16[1,128,16,2048]{3,1,2,0:T(8,128)(2,1)}) %all-gather.3.cloned.1.call-update) | async-done | bytes 8388624 | tf_op jit(solution)/shard_map/all_gather | solution.py:84
  194.9 3.7 fusion.51
  207.0 2.5 convert_reduce_fusion
  209.6 3.7 collective-permute-start.2
  213.3 1.9 collective-permute-start.3
  216.6 4.4 collective-permute-done.3
  222.1 31.8 %psum.15 = f32[16]{0:T(128)} all-reduce(f32[16]{0:T(128)S(1)} %get-tuple-element.10), channel_id=1, replica_groups=mesh['rows'=16,'chan'=8] {'rows'}, use_global_device_ids=true, to_apply=%region_2.3 | all-reduce | flops 16 | bytes 128 | tf_op jit(solution)/shard_map/psum | solution.py:94
  253.9 4.1 fusion.129
  258.0 3.6 fusion.125
  261.6 3.9 fusion.135
  265.5 1.8 fusion.141
  268.5 1.8 fusion.147
  270.3 1.8 fusion.153
  273.3 2.0 fusion.159
  276.0 118.1 %all-gather.5.cloned.1.call-done = bf16[1,128,16,2048]{3,1,2,0:T(8,128)(2,1)} async-done(((bf16[1,16,16,2048]{3,1,2,0:T(8,128)(2,1)}), bf16[1,128,16,2048]{3,1,2,0:T(8,128)(2,1)}) %all-gather.5.cloned.1.call-update) | async-done | bytes 8388624 | tf_op jit(solution)/shard_map/all_gather | solution.py:89
  394.1 3.8 fusion.23
  398.8 1.4 fusion.21
  401.6 1.4 fusion.17
  406.7 1.6 fusion.117
  409.4 115.9 %all-reduce.4.cloned.1.call-done = f32[9,16,128]{2,1,0:T(8,128)} async-done(((f32[9,16,128]{2,1,0:T(8,128)}), f32[9,16,128]{2,1,0:T(8,128)}) %all-reduce.4.cloned.1.call-update) | async-done | bytes 73744 | tf_op jit(solution)/shard_map/psum | solution.py:94
  525.4 1.5 copy.33
  (44 shorter events, 25.9 us)
Async XLA Ops:
  7.2 187.7 %copy-start = (bf16[9,128,128]{2,1,0:T(8,128)(2,1)S(1)}, bf16[9,128,128]{2,1,0:T(8,128)(2,1)}, u32[]{:S(2)}) copy-start(bf16[9,128,128]{2,1,0:T(8,128)(2,1)} %param.6) | copy-start | bytes 884740
  7.2 187.7 %all-gather.3.cloned.1.call-start = ((), (), s32[]{:S(2)}) async-start(), calls=%async_computation | async-start | bytes 9437184 | tf_op jit(solution)/shard_map/all_gather | solution.py:84
  8.6 7.8 %collective-permute-start = (bf16[1,16,4,2048]{3,1,2,0:T(8,128)(2,1)S(1)}, bf16[1,16,4,2048]{3,1,2,0:T(8,128)(2,1)S(1)}, u32[]{:S(2)}, u32[]{:S(2)}) collective-permute-start(bf16[1,16,4,2048]{3,1,2,0:T(8,128)(2,1)S(1)} %get-tuple-element.8), channel_id=1, source_target_pairs={{0,8},{8,16},{16,24},{24,32},{32,40},{40,48},{48,56},{56,64},{64,7... | collective-permute-start | bytes 786440 | tf_op jit(solution)/shard_map/ppermute | solution.py:12
  13.2 7.7 %collective-permute-start.1 = (bf16[1,16,4,2048]{3,1,2,0:T(8,128)(2,1)S(1)}, bf16[1,16,4,2048]{3,1,2,0:T(8,128)(2,1)S(1)}, u32[]{:S(2)}, u32[]{:S(2)}) collective-permute-start(bf16[1,16,4,2048]{3,1,2,0:T(8,128)(2,1)S(1)} %get-tuple-element.9), channel_id=1, source_target_pairs={{8,0},{16,8},{24,16},{32,24},{40,32},{48,40},{56,48},{64,56},{72,6... | collective-permute-start | bytes 786440 | tf_op jit(solution)/shard_map/ppermute | solution.py:15
  22.1 372.1 %all-gather.5.cloned.1.call-start = ((), (), s32[]{:S(2)}) async-start(), calls=%async_computation.1 | async-start | bytes 9437184 | tf_op jit(solution)/shard_map/all_gather | solution.py:89
  194.9 4.6 copy-start.1
  205.0 2.0 copy-start.3
  209.6 7.0 %collective-permute-start.2 = (bf16[1,16,4,2048]{3,1,2,0:T(8,128)(2,1)S(1)}, bf16[1,16,4,2048]{3,1,2,0:T(8,128)(2,1)S(1)}, u32[]{:S(2)}, u32[]{:S(2)}) collective-permute-start(bf16[1,16,4,2048]{3,1,2,0:T(8,128)(2,1)S(1)} %get-tuple-element.6), channel_id=1, source_target_pairs={{0,8},{8,16},{16,24},{24,32},{32,40},{40,48},{48,56},{56,64},{64,7... | collective-permute-start | bytes 786440 | tf_op jit(solution)/shard_map/ppermute | solution.py:12
  213.3 7.7 %collective-permute-start.3 = (bf16[1,16,4,2048]{3,1,2,0:T(8,128)(2,1)S(1)}, bf16[1,16,4,2048]{3,1,2,0:T(8,128)(2,1)S(1)}, u32[]{:S(2)}, u32[]{:S(2)}) collective-permute-start(bf16[1,16,4,2048]{3,1,2,0:T(8,128)(2,1)S(1)} %get-tuple-element.7), channel_id=1, source_target_pairs={{8,0},{16,8},{24,16},{32,24},{40,32},{48,40},{56,48},{64,56},{72,6... | collective-permute-start | bytes 786440 | tf_op jit(solution)/shard_map/ppermute | solution.py:15
  222.1 303.3 %all-reduce.4.cloned.1.call-start = ((), (), s32[]{:S(2)}) async-start(), calls=%async_computation.2 | async-start | bytes 147456 | tf_op jit(solution)/shard_map/psum | solution.py:94
  253.9 11.6 %slice-start = ((s8[8388608]{0:T(1024)(128)(4,1)}), s8[4194304]{0:T(1024)(128)(4,1)S(1)}, s32[]{:S(2)}) async-start(s8[8388608]{0:T(1024)(128)(4,1)} %bitcast.308), calls=%async_computation.3 | async-start | bytes 8388608
  258.0 7.5 %slice-start.1 = ((s8[8388608]{0:T(1024)(128)(4,1)}), s8[4194304]{0:T(1024)(128)(4,1)S(1)}, s32[]{:S(2)}) async-start(s8[8388608]{0:T(1024)(128)(4,1)} %bitcast.308), calls=%async_computation.4 | async-start | bytes 8388608
  275.3 0.7 copy-start.4
  394.1 4.6 copy-start.2
Sparse Core Ops, SparseCore 0:
  22.2 172.6 all-gather.2
  222.2 171.8 all-gather.4
  397.2 128.1 all-reduce.3
where the time goes:
time: 534 us; the launch traced here: 533 us
  waiting for transfers between devices  418 us (78%)
  matrix products  48.4 us (9%)
  blocking collectives  31.8 us (6%)
  between operations  13.9 us (3%)
  starting transfers between devices  12.1 us (2%)
  local copies, waits for them, and re-layouts  7.28 us (1%)
    all_gather x1, waiting for transfers between devices, shards(): act_all = lax.all_gather(act_rim, 'chan', axis=1, tiled=True)  172 us
    all_gather x1, waiting for transfers between devices, shards(): delta_all = lax.all_gather(delta_rim, 'chan', axis=1, tiled=True)  118 us
    psum x1, waiting for transfers between devices, shards(): weight_grad, bias_grad = lax.psum((kern_part, bias_part), 'rows')  116 us
    psum x1, blocking collectives, shards(): weight_grad, bias_grad = lax.psum((kern_part, bias_part), 'rows')  31.8 us
    dot_general x9, matrix products, kernel_taps(): jnp.einsum('bohw,bihw->oi', delta, window, preferred_element_type=jnp.flo...  21.4 us
    dot_general x9, matrix products, forward_taps(): jnp.einsum('oi,bihw->bohw', kernel[3 * tap_row + tap_col], window, prefer...  13.7 us
    dot_general x9, matrix products, backward_taps(): jnp.einsum('oi,bohw->bihw', kernel[3 * tap_row + tap_col], back, preferre...  13.3 us
  transfers between devices with their start and end apart: 7, of which 7 were waited for; matrix products, arithmetic and copies ran while one was open for 7% of the time, Pallas kernels for 0%

commit v1 on v0

v1 whole, which is shorter than its diff:
```python
import functools

import jax
import jax.numpy as jnp
from jax import lax
from jax.experimental import pallas as pl
from jax.experimental.pallas import tpu as pltpu
from jax.sharding import PartitionSpec as P

MESH = pl.DeviceIdType.MESH
F32 = jnp.float32
BF16 = jnp.bfloat16

CH = 128
OWN = 16
PEERS = 8
COLS = 512
PIECES = 10


def wait_bytes(ref, sem):
    pltpu.make_async_copy(ref, ref, sem).wait()


def column_phases():
    w = lax.broadcasted_iota(jnp.int32, (COLS, COLS), 0)
    m = lax.broadcasted_iota(jnp.int32, (COLS, COLS), 1)
    return jnp.where(w == 4 * (m & 127) + (m >> 7), 1.0, 0.0).astype(BF16)


def split_phases(block, perm, tmp, send):
    for b in range(4):
        x = block[:, :, COLS * b : COLS * (b + 1)].astype(F32).reshape(CH, COLS).astype(BF16)
        y = jnp.dot(x, perm[...], preferred_element_type=F32)
        for phase in range(4):
            tmp[4 * b + phase] = y[:, 128 * phase : 128 * (phase + 1)]
    for b in range(4):
        for phase in range(4):
            for h in range(8):
                f, half, k = h % 2, (h % 4) // 2, h // 4
                rows = tmp[4 * b + phase, pl.ds(h, OWN, stride=8), :]
                send[f, 2 * phase + half, k, :, 128 * b : 128 * (b + 1)] = rows.astype(BF16)


def stack_shifts(src, dst, ahead):
    def body(i, carry):
        at = pl.multiple_of(i * 32, 32)
        x = src[pl.ds(at, 32), :]
        lane = lax.broadcasted_iota(jnp.int32, (32, COLS), 1)
        xf = x.astype(F32)
        later = jnp.where(lane == 0, 0.0, pltpu.roll(xf, 1, 1)).astype(BF16)
        earlier = jnp.where(lane == COLS - 1, 0.0, pltpu.roll(xf, COLS - 1, 1)).astype(BF16)
        first, last = (earlier, later) if ahead else (later, earlier)
        dst[pl.ds(at, 32), :] = first
        dst[pl.ds(at + 128, 32), :] = x
        dst[pl.ds(at + 256, 32), :] = last
        return carry

    lax.fori_loop(0, CH // 32, body, 0)


def kernel(
    ranks,
    act_ref,
    og_ref,
    w_ref,
    bias_ref,
    gin_ref,
    wg_ref,
    bg_ref,
    act_v,
    og_v,
    perm,
    tmp,
    act_s,
    og_s,
    act_a,
    og_a,
    act_x,
    delta_a,
    delta_x,
    w_fwd,
    w_bwd,
    total,
    gin_s,
    gin_r,
    back,
    out_v,
    wg_acc,
    b_acc,
    wg_s,
    wg_r,
    part,
    part_r,
    full,
    load_sem,
    a2a_send,
    a2a_recv,
    halo_send,
    halo_recv,
    ret_send,
    ret_recv,
    wg_send,
    wg_recv,
    part_send,
    part_recv,
    full_send,
    full_recv,
    out_sem,
):
    r = lax.axis_index("rows")
    c = lax.axis_index("chan")
    c16 = pl.multiple_of(c * OWN, OWN)
    dot = functools.partial(jnp.dot, preferred_element_type=F32)

    load_act = pltpu.make_async_copy(act_ref, act_v, load_sem.at[0])
    load_og = pltpu.make_async_copy(og_ref, og_v, load_sem.at[1])
    load_act.start()
    load_og.start()
    for p in range(3):
        for q in range(3):
            pltpu.make_async_copy(
                w_ref.at[3 * p + q],
                w_fwd.at[pl.ds(128 * p, 128), pl.ds(128 * q, 128)],
                load_sem.at[2],
            ).start()

    barrier = pltpu.get_barrier_semaphore()

    def greet_chan(s, carry):
        pl.semaphore_signal(
            barrier, inc=1, device_id={"chan": lax.rem(c + s, PEERS)}, device_id_type=MESH
        )
        return carry

    def greet_rows(s, carry):
        pl.semaphore_signal(
            barrier, inc=1, device_id={"rows": lax.rem(r + s, ranks)}, device_id_type=MESH
        )
        return carry

    lax.fori_loop(1, PEERS, greet_chan, 0)
    lax.fori_loop(1, ranks, greet_rows, 0)

    perm[...] = column_phases()
    load_act.wait()
    split_phases(act_v, perm, tmp, act_s)

    pl.semaphore_wait(barrier, PEERS - 1 + ranks - 1)

    def exchange(kind, f, send, land, rows):
        def step(s, carry):
            to = lax.rem(c + s, PEERS)
            pltpu.make_async_remote_copy(
                src_ref=send.at[f, to],
                dst_ref=land.at[f, rows, pl.ds(c16, OWN), :],
                send_sem=a2a_send.at[2 * kind + f],
                recv_sem=a2a_recv.at[2 * kind + f],
                device_id={"chan": to},
                device_id_type=MESH,
            ).start()
            return carry

        lax.fori_loop(1, PEERS, step, 0)
        pltpu.make_async_copy(
            send.at[f, c], land.at[f, rows, pl.ds(c16, OWN), :], a2a_recv.at[2 * kind + f]
        ).start()

    def halo_copy(buf, kind, f, down):
        at = 2 * (2 * kind + f) + down
        return pltpu.make_async_remote_copy(
            src_ref=buf.at[f, 2 if down else 1],
            dst_ref=buf.at[f, 0 if down else 3],
            send_sem=halo_send.at[at],
            recv_sem=halo_recv.at[at],
            device_id={"rows": lax.rem(r + (1 if down else ranks - 1), ranks)},
            device_id_type=MESH,
        )

    def send_halos(buf, kind, f):
        @pl.when(r < ranks - 1)
        def _():
            halo_copy(buf, kind, f, 1).start()

        @pl.when(r > 0)
        def _():
            halo_copy(buf, kind, f, 0).start()

    def wait_halos(buf, kind, f):
        @pl.when(r > 0)
        def _():
            halo_copy(buf, kind, f, 1).wait_recv()

        @pl.when(r == 0)
        def _():
            buf[f, 0] = jnp.zeros((CH, COLS), BF16)

        @pl.when(r < ranks - 1)
        def _():
            halo_copy(buf, kind, f, 0).wait_recv()

        @pl.when(r == ranks - 1)
        def _():
            buf[f, 3] = jnp.zeros((CH, COLS), BF16)

    own = pl.ds(1, 2)
    both = pl.ds(0, 2)
    exchange(0, 0, act_s, act_a, own)
    load_og.wait()
    split_phases(og_v, perm, tmp, og_s)
    exchange(1, 0, og_s, og_a, both)
    exchange(0, 1, act_s, act_a, own)
    exchange(1, 1, og_s, og_a, both)

    wait_bytes(w_fwd, load_sem.at[2])
    for p in range(3):
        for q in range(3):
            at = (pl.ds(128 * p, 128), pl.ds(128 * q, 128))
            w_bwd[at] = w_fwd[at].astype(F32).T.astype(BF16)
    eye = lax.broadcasted_iota(jnp.int32, (CH, CH), 0) == lax.broadcasted_iota(
        jnp.int32, (CH, CH), 1
    )
    bias = jnp.sum(jnp.where(eye, bias_ref[...], 0.0), axis=1, keepdims=True)
    wg_acc[...] = jnp.zeros_like(wg_acc)
    b_acc[...] = jnp.zeros_like(b_acc)

    def taps_own(w, x, f, order):
        keep, up, down = order
        for n in range(2):
            cols = pl.ds(256 * n, 256)
            first = x[f, 1, :, cols]
            second = x[f, 2, :, cols]
            w_keep = w[128 * keep : 128 * keep + 128, :]
            w_up = w[128 * up : 128 * up + 128, :]
            w_down = w[128 * down : 128 * down + 128, :]
            total[0, :, cols] = dot(w_keep, first) + dot(w_down, second)
            total[1, :, cols] = dot(w_up, first) + dot(w_keep, second)

    def taps_halo(w, x, f, order):
        keep, up, down = order
        for n in range(2):
            cols = pl.ds(256 * n, 256)
            total[0, :, cols] += dot(w[128 * up : 128 * up + 128, :], x[f, 0, :, cols])
            total[1, :, cols] += dot(w[128 * down : 128 * down + 128, :], x[f, 3, :, cols])

    forward = (1, 0, 2)
    backward = (1, 2, 0)

    def start_act(f):
        wait_bytes(act_a.at[f, own], a2a_recv.at[f])
        send_halos(act_a, 0, f)
        for k in (1, 2):
            stack_shifts(act_a.at[f, k], act_x.at[f, k], False)

    def make_delta(f):
        taps_own(w_fwd, act_x, f, forward)
        wait_halos(act_a, 0, f)
        for k in (0, 3):
            stack_shifts(act_a.at[f, k], act_x.at[f, k], False)
        taps_halo(w_fwd, act_x, f, forward)
        wait_bytes(og_a.at[f], a2a_recv.at[2 + f])
        for k in range(2):
            for at in range(0, CH, 16):
                rows = slice(at, at + 16)
                pre = total[k, rows, :] + bias[rows, :]
                s = jax.nn.sigmoid(pre)
                delta = (og_a[f, k, rows, :].astype(F32) * s * (1.0 + pre * (1.0 - s))).astype(BF16)
                delta_a[f, 1 + k, rows, :] = delta
                b_acc[rows, :] += jnp.sum(delta.astype(F32), axis=1, keepdims=True)
        send_halos(delta_a, 1, f)

    def add_weight_grad(f):
        for k in range(2):
            for p in range(3):
                wg_acc[p] += lax.dot_general(
                    delta_a[f, 1 + k],
                    act_x[f, k + p],
                    (((1,), (1,)), ((), ())),
                    preferred_element_type=F32,
                )

    def make_input_grad(f):
        for k in (1, 2):
            stack_shifts(delta_a.at[f, k], delta_x.at[f, k], True)
        taps_own(w_bwd, delta_x, f, backward)
        wait_halos(delta_a, 1, f)
        for k in (0, 3):
            stack_shifts(delta_a.at[f, k], delta_x.at[f, k], True)
        taps_halo(w_bwd, delta_x, f, backward)
        for k in range(2):
            gin_s[f, k] = total[k].astype(BF16)

        def step(s, carry):
            to = lax.rem(c + s, PEERS)
            pltpu.make_async_remote_copy(
                src_ref=gin_s.at[f, :, pl.ds(pl.multiple_of(to * OWN, OWN), OWN), :],
                dst_ref=gin_r.at[f, c],
                send_sem=ret_send.at[f],
                recv_sem=ret_recv.at[f],
                device_id={"chan": to},
                device_id_type=MESH,
            ).start()
            return carry

        lax.fori_loop(1, PEERS, step, 0)
        pltpu.make_async_copy(
            gin_s.at[f, :, pl.ds(c16, OWN), :], gin_r.at[f, c], ret_recv.at[f]
        ).start()

    def send_weight_grad():
        for d in range(PEERS):
            rows = slice(OWN * d, OWN * (d + 1))
            for t in range(9):
                p, q = t // 3, t % 3
                wg_s[d, t] = wg_acc[p, rows, 128 * q : 128 * (q + 1)].astype(BF16)
            wg_s[d, 9] = jnp.broadcast_to(b_acc[rows, :], (OWN, CH)).astype(BF16)

        def step(s, carry):
            to = lax.rem(c + s, PEERS)
            pltpu.make_async_remote_copy(
                src_ref=wg_s.at[to],
                dst_ref=wg_r.at[c],
                send_sem=wg_send,
                recv_sem=wg_recv,
                device_id={"chan": to},
                device_id_type=MESH,
            ).start()
            return carry

        lax.fori_loop(1, PEERS, step, 0)
        pltpu.make_async_copy(wg_s.at[c], wg_r.at[c], wg_recv).start()

    def send_parts():
        wait_bytes(wg_r, wg_recv)
        for t in range(PIECES):
            acc = wg_r[0, t].astype(F32)
            for d in range(1, PEERS):
                acc += wg_r[d, t].astype(F32)
            part[t] = acc
        for t in range(PIECES):
            owner = t % ranks

            @pl.when(r != owner)
            def _():
                pltpu.make_async_remote_copy(
                    src_ref=part.at[t],
                    dst_ref=part_r.at[t, r],
                    send_sem=part_send.at[t],
                    recv_sem=part_recv.at[t],
                    device_id={"rows": owner},
                    device_id_type=MESH,
                ).start()

            @pl.when(r == owner)
            def _():
                pltpu.make_async_copy(part.at[t], part_r.at[t, r], part_recv.at[t]).start()

    def full_copy(t, to):
        return pltpu.make_async_remote_copy(
            src_ref=full.at[t],
            dst_ref=full.at[t],
            send_sem=full_send.at[t],
            recv_sem=full_recv.at[t],
            device_id={"rows": to},
            device_id_type=MESH,
        )

    def send_full():
        for t in range(PIECES):

            @pl.when(r == t % ranks)
            def _():
                wait_bytes(part_r.at[t], part_recv.at[t])
                acc = part_r[t, 0]
                for d in range(1, ranks):
                    acc += part_r[t, d]
                full[t] = acc

                def step(s, carry):
                    full_copy(t, lax.rem(r + s, ranks)).start()
                    return carry

                lax.fori_loop(1, ranks, step, 0)

    def join_phases(f):
        wait_bytes(gin_r.at[f], ret_recv.at[f])
        for b in range(4):
            cols = slice(128 * b, 128 * (b + 1))
            x = jnp.concatenate(
                [
                    jnp.concatenate([gin_r[f, 2 * phase + half, k, :, cols] for phase in range(4)], axis=1)
                    for half in range(2)
                    for k in range(2)
                ],
                axis=0,
            )
            y = lax.dot_general(x, perm[...], (((1,), (1,)), ((), ())), preferred_element_type=F32)
            for half in range(2):
                for k in range(2):
                    h = 4 * k + 2 * half + f
                    at = 16 * (2 * half + k)
                    for n in range(4):
                        back[4 * b + n, OWN * h : OWN * (h + 1), :] = y[
                            at : at + 16, 128 * n : 128 * (n + 1)
                        ]

    def store_input_grad():
        for n in range(16):
            for ch in range(OWN):
                rows = back[n, pl.ds(ch, 8, stride=OWN), :]
                out_v[ch, :, 128 * n : 128 * (n + 1)] = rows.astype(BF16)
        pltpu.make_async_copy(out_v, gin_ref, out_sem.at[0]).start()

    start_act(0)
    make_delta(0)
    start_act(1)
    add_weight_grad(0)
    make_delta(1)
    make_input_grad(0)
    add_weight_grad(1)
    send_weight_grad()
    make_input_grad(1)
    send_parts()
    join_phases(0)
    send_full()
    join_phases(1)
    store_input_grad()

    for t in range(PIECES):

        @pl.when(r != t % ranks)
        def _():
            full_copy(t, r).wait_recv()

    out_w = pltpu.make_async_copy(full.at[pl.ds(0, 9)], wg_ref, out_sem.at[1])
    out_b = pltpu.make_async_copy(full.at[9], bg_ref, out_sem.at[2])
    out_w.start()
    out_b.start()

    for f in range(2):
        wait_bytes(act_s.at[f, pl.ds(0, PEERS - 1)], a2a_send.at[f])
        wait_bytes(og_s.at[f, pl.ds(0, PEERS - 1)], a2a_send.at[2 + f])
        wait_bytes(gin_r.at[f, pl.ds(0, PEERS - 1)], ret_send.at[f])
    wait_bytes(wg_s.at[pl.ds(0, PEERS - 1)], wg_send)
    for kind, buf in ((0, act_a), (1, delta_a)):
        for f in range(2):

            @pl.when(r < ranks - 1)
            def _():
                halo_copy(buf, kind, f, 1).wait_send()

            @pl.when(r > 0)
            def _():
                halo_copy(buf, kind, f, 0).wait_send()

    for t in range(PIECES):

        @pl.when(r != t % ranks)
        def _():
            wait_bytes(part.at[t], part_send.at[t])

        @pl.when(r == t % ranks)
        def _():
            wait_bytes(part_r.at[t, pl.ds(0, ranks - 1)], full_send.at[t])

    pltpu.make_async_copy(out_v, gin_ref, out_sem.at[0]).wait()
    out_w.wait()
    out_b.wait()


def fused(ranks, activation, out_grad, weights, biases):
    height = activation.shape[1]
    extent = activation.shape[2]
    vmem = pltpu.VMEM
    dma = pltpu.SemaphoreType.DMA
    return pl.pallas_call(
        functools.partial(kernel, ranks),
        out_shape=(
            jax.ShapeDtypeStruct((OWN, height, extent), BF16),
            jax.ShapeDtypeStruct((9, OWN, CH), F32),
            jax.ShapeDtypeStruct((OWN, CH), F32),
        ),
        in_specs=[
            pl.BlockSpec(memory_space=pl.ANY),
            pl.BlockSpec(memory_space=pl.ANY),
            pl.BlockSpec(memory_space=pl.ANY),
            pl.BlockSpec(memory_space=pltpu.VMEM),
        ],
        out_specs=[pl.BlockSpec(memory_space=pl.ANY)] * 3,
        scratch_shapes=[
            vmem((OWN, height, extent), BF16),
            vmem((OWN, height, extent), BF16),
            vmem((COLS, COLS), BF16),
            vmem((16, CH, 128), F32),
            vmem((2, PEERS, 2, OWN, COLS), BF16),
            vmem((2, PEERS, 2, OWN, COLS), BF16),
            vmem((2, 4, CH, COLS), BF16),
            vmem((2, 2, CH, COLS), BF16),
            vmem((2, 4, 3 * CH, COLS), BF16),
            vmem((2, 4, CH, COLS), BF16),
            vmem((2, 4, 3 * CH, COLS), BF16),
            vmem((3 * CH, 3 * CH), BF16),
            vmem((3 * CH, 3 * CH), BF16),
            vmem((2, CH, COLS), F32),
            vmem((2, 2, CH, COLS), BF16),
            vmem((2, PEERS, 2, OWN, COLS), BF16),
            vmem((16, CH, 128), F32),
            vmem((OWN, height, extent), BF16),
            vmem((3, CH, 3 * CH), F32),
            vmem((CH, 1), F32),
            vmem((PEERS, PIECES, OWN, CH), BF16),
            vmem((PEERS, PIECES, OWN, CH), BF16),
            vmem((PIECES, OWN, CH), F32),
            vmem((PIECES, ranks, OWN, CH), F32),
            vmem((PIECES, OWN, CH), F32),
            dma((3,)),
            dma((4,)),
            dma((4,)),
            dma((8,)),
            dma((8,)),
            dma((2,)),
            dma((2,)),
            dma,
            dma,
            dma((PIECES,)),
            dma((PIECES,)),
            dma((PIECES,)),
            dma((PIECES,)),
            dma((3,)),
        ],
        compiler_params=pltpu.CompilerParams(
            collective_id=0, has_side_effects=True, vmem_limit_bytes=48 * 1024 * 1024
        ),
        name="conv_backward",
    )(activation, out_grad, weights, biases)


def shards(ranks, activation, out_grad, weights, biases):
    gin, wg, bg = fused(
        ranks, activation[0], out_grad[0], weights, biases.reshape(1, CH)
    )
    return gin[None], wg, bg[:, 0]


def solution(mesh):
    return jax.shard_map(
        functools.partial(shards, mesh.shape["rows"]),
        mesh=mesh,
        in_specs=(P(None, "chan", "rows", None), P(None, "chan", "rows", None), P(), P()),
        out_specs=(P(None, "chan", "rows", None), P(None, "chan", None), P("chan")),
        check_vma=False,
    )
```

time: 534 us -> 55.8 us (0.10)
  waiting for transfers between devices: 418 us -> 0 us
  Pallas kernels: 0 us -> 49.2 us
  matrix products: 48.4 us -> 0 us
  blocking collectives: 31.8 us -> 0 us
  between operations: 13.9 us -> 0.65 us
  starting transfers between devices: 12.1 us -> 0 us
    all_gather x2 -> x0, waiting for transfers between devices: 290 us -> none  [the longest x1 172 us: shards(): act_all = lax.all_gather(act_rim, 'chan', axis=1, tiled=True)]
    psum x1 -> x0, waiting for transfers between devices: 116 us -> none  [shards(): weight_grad, bias_grad = lax.psum((kern_part, bias_part), 'rows')]
    pallas_call x0 -> x1, Pallas kernels: none -> 49.2 us  [fused(): pl.pallas_call(functools.partial(kernel, ranks), out_shape=(jax.ShapeDtyp...]
    dot_general x27 -> x0, matrix products: 48.4 us -> none  [the longest x9 21.4 us: kernel_taps(): jnp.einsum('bohw,bihw->oi', delta, window, preferred_element_type=jnp.flo...]
    psum x1 -> x0, blocking collectives: 31.8 us -> none  [shards(): weight_grad, bias_grad = lax.psum((kern_part, bias_part), 'rows')]
    ppermute x4 -> x0, starting transfers between devices: 12 us -> none  [the longest x2 8.17 us: extended(): lax.ppermute(lax.slice_in_dim(block, block.shape[dim] - width, None, axis...]
    ppermute x4 -> x0, waiting for transfers between devices: 11.5 us -> none  [the longest x2 8.79 us: extended(): lax.ppermute(lax.slice_in_dim(block, 0, width, axis=dim), axis, backward)]
  transfers between devices with their start and end apart: 7 -> 0, of which waited for: 7 -> 0; matrix products, arithmetic and copies ran while one was open for 7% -> 0% of each run, Pallas kernels for 0% -> 0%
where the time goes in v1:
time: 55.8 us; the launch traced here: 55.6 us
  Pallas kernels  49.2 us (88%)
  local copies, waits for them, and re-layouts  5.74 us (10%)
  between operations  0.65 us (1%)
    pallas_call x1, Pallas kernels, fused(): pl.pallas_call(functools.partial(kernel, ranks), out_shape=(jax.ShapeDtyp...  49.2 us
    unnamed x10, local copies, waits for them, and re-layouts  5.12 us

profile of v1, /device:TPU:1, one launch (start us, length us, event | category | flops | bytes accessed | tf_op | source)
XLA Modules:
  0.0 55.6 jit_solution(999095526429515873)
XLA Ops:
  0.6 0.0 copy-start.3
  0.6 0.6 %copy-done.3 = f32[128]{0:T(128)S(1)} copy-done((f32[128]{0:T(128)S(1)}, f32[128]{0:T(128)}, u32[]{:S(2)}) %copy-start.3) | copy-done | bytes 536
  1.3 0.0 copy-start
  1.3 1.0 %copy-done = bf16[1,16,8,2048]{3,2,1,0:T(8,128)(2,1)S(1)} copy-done((bf16[1,16,8,2048]{3,2,1,0:T(8,128)(2,1)S(1)}, bf16[1,16,8,2048]{3,2,1,0:T(8,128)(2,1)}, u32[]{:S(2)}) %copy-start) | copy-done | bytes 524312
  2.3 0.0 copy-start.1
  2.3 1.0 %copy-done.1 = bf16[1,16,8,2048]{3,2,1,0:T(8,128)(2,1)S(1)} copy-done((bf16[1,16,8,2048]{3,2,1,0:T(8,128)(2,1)S(1)}, bf16[1,16,8,2048]{3,2,1,0:T(8,128)(2,1)}, u32[]{:S(2)}) %copy-start.1) | copy-done | bytes 524312
  3.4 0.0 copy-start.2
  3.4 1.0 %copy-done.2 = bf16[9,128,128]{2,1,0:T(8,128)(2,1)S(1)} copy-done((bf16[9,128,128]{2,1,0:T(8,128)(2,1)S(1)}, bf16[9,128,128]{2,1,0:T(8,128)(2,1)}, u32[]{:S(2)}) %copy-start.2) | copy-done | bytes 294936
  4.3 49.2 %conv_backward.1 = (bf16[16,8,2048]{2,1,0:T(8,128)(2,1)S(1)}, f32[9,16,128]{2,1,0:T(8,128)S(1)}, f32[16,128]{1,0:T(8,128)S(1)}) custom-call(bf16[16,8,2048]{2,1,0:T(8,128)(2,1)S(1)} %bitcast.4, bf16[16,8,2048]{2,1,0:T(8,128)(2,1)S(1)} %bitcast.5, bf16[9,128,128]{2,1,0:T(8,128)(2,1)S(1)} %copy-done.2, f32[1,128]{1,0:T(1,128)S(1)} %bitcast.7), custom_call_target="tpu_custom_call" | custom-call | tf_op jit(solution)/shard_map/conv_backward/pallas_call | solution.py:476
  53.5 0.6 %slice_reduce_fusion = f32[16]{0:T(128)} fusion(f32[16,128]{1,0:T(8,128)S(1)} %get-tuple-element.8), kind=kLoop, calls=%fused_computation | loop fusion | bytes 128 | tf_op jit(solution)/shard_map/slice | solution.py:542
  54.1 0.8 %copy.9 = bf16[1,16,8,2048]{3,2,1,0:T(8,128)(2,1)} copy(bf16[1,16,8,2048]{3,2,1,0:T(8,128)(2,1)S(1)} %bitcast.6) | data formatting | bytes 1048576
  54.9 0.6 %copy.10 = f32[9,16,128]{2,1,0:T(8,128)} copy(f32[9,16,128]{2,1,0:T(8,128)S(1)} %get-tuple-element.13) | data formatting | bytes 147456
Async XLA Ops:
  0.6 0.7 %copy-start.3 = (f32[128]{0:T(128)S(1)}, f32[128]{0:T(128)}, u32[]{:S(2)}) copy-start(f32[128]{0:T(128)} %param.7) | copy-start | bytes 1540
  1.3 1.0 %copy-start = (bf16[1,16,8,2048]{3,2,1,0:T(8,128)(2,1)S(1)}, bf16[1,16,8,2048]{3,2,1,0:T(8,128)(2,1)}, u32[]{:S(2)}) copy-start(bf16[1,16,8,2048]{3,2,1,0:T(8,128)(2,1)} %param.4) | copy-start | bytes 1572868
  2.3 1.0 %copy-start.1 = (bf16[1,16,8,2048]{3,2,1,0:T(8,128)(2,1)S(1)}, bf16[1,16,8,2048]{3,2,1,0:T(8,128)(2,1)}, u32[]{:S(2)}) copy-start(bf16[1,16,8,2048]{3,2,1,0:T(8,128)(2,1)} %param.5) | copy-start | bytes 1572868
  3.4 1.0 %copy-start.2 = (bf16[9,128,128]{2,1,0:T(8,128)(2,1)S(1)}, bf16[9,128,128]{2,1,0:T(8,128)(2,1)}, u32[]{:S(2)}) copy-start(bf16[9,128,128]{2,1,0:T(8,128)(2,1)} %w_ref.1) | copy-start | bytes 884740

commit v2 on v1

--- a/solution.py
+++ b/solution.py
@@ -16,10 +16,26 @@
 PEERS = 8
 COLS = 512
 PIECES = 10
+HELD = 3
 
 
 def wait_bytes(ref, sem):
     pltpu.make_async_copy(ref, ref, sem).wait()
+
+
+def remote(src, dst, send_sem, recv_sem, device):
+    return pltpu.make_async_remote_copy(
+        src_ref=src,
+        dst_ref=dst,
+        send_sem=send_sem,
+        recv_sem=recv_sem,
+        device_id=device,
+        device_id_type=MESH,
+    )
+
+
+def local(src, dst, sem):
+    return pltpu.make_async_copy(src, dst, sem)
 
 
 def column_phases():
@@ -56,7 +72,7 @@
         dst[pl.ds(at + 256, 32), :] = last
         return carry
 
-    lax.fori_loop(0, CH // 32, body, 0)
+    lax.fori_loop(0, CH // 32, body, 0, unroll=True)
 
 
 def kernel(
@@ -104,13 +120,25 @@
     wg_recv,
     part_send,
     part_recv,
-    full_send,
-    full_recv,
     out_sem,
 ):
     r = lax.axis_index("rows")
     c = lax.axis_index("chan")
     c16 = pl.multiple_of(c * OWN, OWN)
+    far = r // (ranks // 2)
+
+    xs = ranks // 4
+    x = lax.rem(r // 2, xs)
+
+    def first_piece(at):
+        return HELD * at - (HELD * xs - PIECES) * (at // (xs - 1))
+
+    def flipped(at):
+        return at + 1 - 2 * lax.rem(at, 2)
+
+    def slot_of(at):
+        return at + far * (flipped(at) - at)
+
     dot = functools.partial(jnp.dot, preferred_element_type=F32)
 
     load_act = pltpu.make_async_copy(act_ref, act_v, load_sem.at[0])
@@ -141,41 +169,51 @@
 
     lax.fori_loop(1, PEERS, greet_chan, 0)
     lax.fori_loop(1, ranks, greet_rows, 0)
+    border = ranks // 2 - 1 + far
+
+    @pl.when(r == border)
+    def _():
+        pl.semaphore_signal(
+            barrier,
+            inc=1,
+            device_id={"rows": ranks - 1 - border, "chan": flipped(c)},
+            device_id_type=MESH,
+        )
+
 
     perm[...] = column_phases()
     load_act.wait()
     split_phases(act_v, perm, tmp, act_s)
 
-    pl.semaphore_wait(barrier, PEERS - 1 + ranks - 1)
+    greeted = PEERS - 1 + ranks - 1
+
+    @pl.when(r == border)
+    def _():
+        pl.semaphore_wait(barrier, greeted + 1)
+
+    @pl.when(r != border)
+    def _():
+        pl.semaphore_wait(barrier, greeted)
 
     def exchange(kind, f, send, land, rows):
         def step(s, carry):
             to = lax.rem(c + s, PEERS)
-            pltpu.make_async_remote_copy(
-                src_ref=send.at[f, to],
-                dst_ref=land.at[f, rows, pl.ds(c16, OWN), :],
-                send_sem=a2a_send.at[2 * kind + f],
-                recv_sem=a2a_recv.at[2 * kind + f],
-                device_id={"chan": to},
-                device_id_type=MESH,
-            ).start()
+            remote(send.at[f, slot_of(to)], land.at[f, rows, pl.ds(c16, OWN), :], a2a_send.at[2 * kind + f], a2a_recv.at[2 * kind + f], {"chan": to}).start()
             return carry
 
         lax.fori_loop(1, PEERS, step, 0)
-        pltpu.make_async_copy(
-            send.at[f, c], land.at[f, rows, pl.ds(c16, OWN), :], a2a_recv.at[2 * kind + f]
+        local(
+            send.at[f, slot_of(c)], land.at[f, rows, pl.ds(c16, OWN), :], a2a_recv.at[2 * kind + f]
         ).start()
+
+    def halo_peer(down):
+        to = lax.rem(r + (1 if down else ranks - 1), ranks)
+        cross = far + to // (ranks // 2) - 2 * far * (to // (ranks // 2))
+        return {"rows": to, "chan": c + cross * (flipped(c) - c)}
 
     def halo_copy(buf, kind, f, down):
         at = 2 * (2 * kind + f) + down
-        return pltpu.make_async_remote_copy(
-            src_ref=buf.at[f, 2 if down else 1],
-            dst_ref=buf.at[f, 0 if down else 3],
-            send_sem=halo_send.at[at],
-            recv_sem=halo_recv.at[at],
-            device_id={"rows": lax.rem(r + (1 if down else ranks - 1), ranks)},
-            device_id_type=MESH,
-        )
+        return remote(buf.at[f, 2 if down else 1], buf.at[f, 0 if down else 3], halo_send.at[at], halo_recv.at[at], halo_peer(down))
 
     def send_halos(buf, kind, f):
         @pl.when(r < ranks - 1)
@@ -206,13 +244,13 @@
     own = pl.ds(1, 2)
     both = pl.ds(0, 2)
     exchange(0, 0, act_s, act_a, own)
+    exchange(0, 1, act_s, act_a, own)
     load_og.wait()
     split_phases(og_v, perm, tmp, og_s)
     exchange(1, 0, og_s, og_a, both)
-    exchange(0, 1, act_s, act_a, own)
     exchange(1, 1, og_s, og_a, both)
 
-    wait_bytes(w_fwd, load_sem.at[2])
+    pltpu.make_async_copy(w_fwd, w_fwd, load_sem.at[2]).wait()
     for p in range(3):
         for q in range(3):
             at = (pl.ds(128 * p, 128), pl.ds(128 * q, 128))
@@ -233,15 +271,18 @@
             w_keep = w[128 * keep : 128 * keep + 128, :]
             w_up = w[128 * up : 128 * up + 128, :]
             w_down = w[128 * down : 128 * down + 128, :]
-            total[0, :, cols] = dot(w_keep, first) + dot(w_down, second)
-            total[1, :, cols] = dot(w_up, first) + dot(w_keep, second)
+            total[f, 0, :, cols] = dot(w_keep, first) + dot(w_down, second)
+            total[f, 1, :, cols] = dot(w_up, first) + dot(w_keep, second)
 
     def taps_halo(w, x, f, order):
         keep, up, down = order
         for n in range(2):
             cols = pl.ds(256 * n, 256)
-            total[0, :, cols] += dot(w[128 * up : 128 * up + 128, :], x[f, 0, :, cols])
-            total[1, :, cols] += dot(w[128 * down : 128 * down + 128, :], x[f, 3, :, cols])
+            total[f, 0, :, cols] += dot(w[128 * up : 128 * up + 128, :], x[f, 0, :, cols])
+            total[f, 1, :, cols] += dot(w[128 * down : 128 * down + 128, :], x[f, 3, :, cols])
+
+    out_w = pltpu.make_async_copy(full.at[pl.ds(0, 9)], wg_ref, out_sem.at[1])
+    out_b = pltpu.make_async_copy(full.at[9], bg_ref, out_sem.at[2])
 
     forward = (1, 0, 2)
     backward = (1, 2, 0)
@@ -252,17 +293,20 @@
         for k in (1, 2):
             stack_shifts(act_a.at[f, k], act_x.at[f, k], False)
 
-    def make_delta(f):
         taps_own(w_fwd, act_x, f, forward)
+
+    def finish_pre(f):
         wait_halos(act_a, 0, f)
         for k in (0, 3):
             stack_shifts(act_a.at[f, k], act_x.at[f, k], False)
         taps_halo(w_fwd, act_x, f, forward)
+
+    def make_delta(f):
         wait_bytes(og_a.at[f], a2a_recv.at[2 + f])
         for k in range(2):
             for at in range(0, CH, 16):
                 rows = slice(at, at + 16)
-                pre = total[k, rows, :] + bias[rows, :]
+                pre = total[f, k, rows, :] + bias[rows, :]
                 s = jax.nn.sigmoid(pre)
                 delta = (og_a[f, k, rows, :].astype(F32) * s * (1.0 + pre * (1.0 - s))).astype(BF16)
                 delta_a[f, 1 + k, rows, :] = delta
@@ -279,32 +323,27 @@
                     preferred_element_type=F32,
                 )
 
-    def make_input_grad(f):
+    def start_input_grad(f):
         for k in (1, 2):
             stack_shifts(delta_a.at[f, k], delta_x.at[f, k], True)
         taps_own(w_bwd, delta_x, f, backward)
+
+    def make_input_grad(f):
         wait_halos(delta_a, 1, f)
         for k in (0, 3):
             stack_shifts(delta_a.at[f, k], delta_x.at[f, k], True)
         taps_halo(w_bwd, delta_x, f, backward)
         for k in range(2):
-            gin_s[f, k] = total[k].astype(BF16)
+            gin_s[f, k] = total[f, k].astype(BF16)
 
         def step(s, carry):
             to = lax.rem(c + s, PEERS)
-            pltpu.make_async_remote_copy(
-                src_ref=gin_s.at[f, :, pl.ds(pl.multiple_of(to * OWN, OWN), OWN), :],
-                dst_ref=gin_r.at[f, c],
-                send_sem=ret_send.at[f],
-                recv_sem=ret_recv.at[f],
-                device_id={"chan": to},
-                device_id_type=MESH,
-            ).start()
+            remote(gin_s.at[f, :, pl.ds(pl.multiple_of(to * OWN, OWN), OWN), :], gin_r.at[f, slot_of(c)], ret_send.at[f], ret_recv.at[f], {"chan": to}).start()
             return carry
 
         lax.fori_loop(1, PEERS, step, 0)
-        pltpu.make_async_copy(
-            gin_s.at[f, :, pl.ds(c16, OWN), :], gin_r.at[f, c], ret_recv.at[f]
+        local(
+            gin_s.at[f, :, pl.ds(c16, OWN), :], gin_r.at[f, slot_of(c)], ret_recv.at[f]
         ).start()
 
     def send_weight_grad():
@@ -315,72 +354,55 @@
                 wg_s[d, t] = wg_acc[p, rows, 128 * q : 128 * (q + 1)].astype(BF16)
             wg_s[d, 9] = jnp.broadcast_to(b_acc[rows, :], (OWN, CH)).astype(BF16)
 
+        def piece_copy(x_to, to):
+            return remote(
+                wg_s.at[to, pl.ds(first_piece(x_to), HELD)],
+                wg_r.at[x * PEERS + c],
+                wg_send,
+                wg_recv,
+                {"rows": r + 2 * (x_to - x), "chan": to},
+            )
+
+        for dx in range(xs):
+            x_to = lax.rem(x + dx, xs)
+
+            def step(s, carry):
+                piece_copy(x_to, lax.rem(c + s, PEERS)).start()
+                return carry
+
+            lax.fori_loop(1 if dx == 0 else 0, PEERS, step, 0)
+        local(wg_s.at[c, pl.ds(first_piece(x), HELD)], wg_r.at[x * PEERS + c], wg_recv).start()
+
+    def send_parts():
+        wait_bytes(wg_r, wg_recv)
+        for t in range(HELD):
+            acc = wg_r[0, t].astype(F32)
+            for d in range(1, xs * PEERS):
+                acc += wg_r[d, t].astype(F32)
+            part[t] = acc.astype(BF16)
+
         def step(s, carry):
-            to = lax.rem(c + s, PEERS)
-            pltpu.make_async_remote_copy(
-                src_ref=wg_s.at[to],
-                dst_ref=wg_r.at[c],
-                send_sem=wg_send,
-                recv_sem=wg_recv,
-                device_id={"chan": to},
-                device_id_type=MESH,
+            remote(
+                part, part_r.at[r], part_send, part_recv, {"rows": lax.rem(r + s, ranks)}
             ).start()
             return carry
 
-        lax.fori_loop(1, PEERS, step, 0)
-        pltpu.make_async_copy(wg_s.at[c], wg_r.at[c], wg_recv).start()
-
-    def send_parts():
-        wait_bytes(wg_r, wg_recv)
+        lax.fori_loop(1, ranks, step, 0)
+        local(part, part_r.at[r], part_recv).start()
+
+    def finish_weight_grad():
+        wait_bytes(part_r, part_recv)
         for t in range(PIECES):
-            acc = wg_r[0, t].astype(F32)
-            for d in range(1, PEERS):
-                acc += wg_r[d, t].astype(F32)
-            part[t] = acc
-        for t in range(PIECES):
-            owner = t % ranks
-
-            @pl.when(r != owner)
-            def _():
-                pltpu.make_async_remote_copy(
-                    src_ref=part.at[t],
-                    dst_ref=part_r.at[t, r],
-                    send_sem=part_send.at[t],
-                    recv_sem=part_recv.at[t],
-                    device_id={"rows": owner},
-                    device_id_type=MESH,
-                ).start()
-
-            @pl.when(r == owner)
-            def _():
-                pltpu.make_async_copy(part.at[t], part_r.at[t, r], part_recv.at[t]).start()
-
-    def full_copy(t, to):
-        return pltpu.make_async_remote_copy(
-            src_ref=full.at[t],
-            dst_ref=full.at[t],
-            send_sem=full_send.at[t],
-            recv_sem=full_recv.at[t],
-            device_id={"rows": to},
-            device_id_type=MESH,
-        )
-
-    def send_full():
-        for t in range(PIECES):
-
-            @pl.when(r == t % ranks)
-            def _():
-                wait_bytes(part_r.at[t], part_recv.at[t])
-                acc = part_r[t, 0]
-                for d in range(1, ranks):
-                    acc += part_r[t, d]
-                full[t] = acc
-
-                def step(s, carry):
-                    full_copy(t, lax.rem(r + s, ranks)).start()
-                    return carry
-
-                lax.fori_loop(1, ranks, step, 0)
+            x_of = min(t // HELD, xs - 1)
+            at = t - first_piece(x_of)
+            held = [
+                part_r[2 * (xs * half + x_of) + core, at].astype(F32)
+                for half in range(2)
+                for core in range(2)
+            ]
+            full[t] = (held[0] + held[1]) + (held[2] + held[3])
+        out_w.start()
+        out_b.start()
 
     def join_phases(f):
         wait_bytes(gin_r.at[f], ret_recv.at[f])
@@ -412,36 +434,30 @@
         pltpu.make_async_copy(out_v, gin_ref, out_sem.at[0]).start()
 
     start_act(0)
+    start_act(1)
+    finish_pre(0)
     make_delta(0)
-    start_act(1)
+    finish_pre(1)
     add_weight_grad(0)
+    start_input_grad(0)
     make_delta(1)
-    make_input_grad(0)
     add_weight_grad(1)
     send_weight_grad()
+    make_input_grad(0)
+    start_input_grad(1)
     make_input_grad(1)
     send_parts()
     join_phases(0)
-    send_full()
     join_phases(1)
     store_input_grad()
-
-    for t in range(PIECES):
-
-        @pl.when(r != t % ranks)
-        def _():
-            full_copy(t, r).wait_recv()
-
-    out_w = pltpu.make_async_copy(full.at[pl.ds(0, 9)], wg_ref, out_sem.at[1])
-    out_b = pltpu.make_async_copy(full.at[9], bg_ref, out_sem.at[2])
-    out_w.start()
-    out_b.start()
+    finish_weight_grad()
 
     for f in range(2):
         wait_bytes(act_s.at[f, pl.ds(0, PEERS - 1)], a2a_send.at[f])
         wait_bytes(og_s.at[f, pl.ds(0, PEERS - 1)], a2a_send.at[2 + f])
         wait_bytes(gin_r.at[f, pl.ds(0, PEERS - 1)], ret_send.at[f])
-    wait_bytes(wg_s.at[pl.ds(0, PEERS - 1)], wg_send)
+    wait_bytes(wg_r.at[pl.ds(0, xs * PEERS - 1)], wg_send)
+    wait_bytes(part_r.at[pl.ds(0, ranks - 1)], part_send)
     for kind, buf in ((0, act_a), (1, delta_a)):
         for f in range(2):
 
@@ -452,16 +468,6 @@
             @pl.when(r > 0)
             def _():
                 halo_copy(buf, kind, f, 0).wait_send()
-
-    for t in range(PIECES):
-
-        @pl.when(r != t % ranks)
-        def _():
-            wait_bytes(part.at[t], part_send.at[t])
-
-        @pl.when(r == t % ranks)
-        def _():
-            wait_bytes(part_r.at[t, pl.ds(0, ranks - 1)], full_send.at[t])
 
     pltpu.make_async_copy(out_v, gin_ref, out_sem.at[0]).wait()
     out_w.wait()
@@ -501,7 +507,7 @@
             vmem((2, 4, 3 * CH, COLS), BF16),
             vmem((3 * CH, 3 * CH), BF16),
             vmem((3 * CH, 3 * CH), BF16),
-            vmem((2, CH, COLS), F32),
+            vmem((2, 2, CH, COLS), F32),
             vmem((2, 2, CH, COLS), BF16),
             vmem((2, PEERS, 2, OWN, COLS), BF16),
             vmem((16, CH, 128), F32),
@@ -509,9 +515,9 @@
             vmem((3, CH, 3 * CH), F32),
             vmem((CH, 1), F32),
             vmem((PEERS, PIECES, OWN, CH), BF16),
-            vmem((PEERS, PIECES, OWN, CH), BF16),
-            vmem((PIECES, OWN, CH), F32),
-            vmem((PIECES, ranks, OWN, CH), F32),
+            vmem((ranks // 4 * PEERS, HELD, OWN, CH), BF16),
+            vmem((HELD, OWN, CH), BF16),
+            vmem((ranks, HELD, OWN, CH), BF16),
             vmem((PIECES, OWN, CH), F32),
             dma((3,)),
             dma((4,)),
@@ -522,14 +528,12 @@
             dma((2,)),
             dma,
             dma,
-            dma((PIECES,)),
-            dma((PIECES,)),
-            dma((PIECES,)),
-            dma((PIECES,)),
+            dma,
+            dma,
             dma((3,)),
         ],
         compiler_params=pltpu.CompilerParams(
-            collective_id=0, has_side_effects=True, vmem_limit_bytes=48 * 1024 * 1024
+            collective_id=0, has_side_effects=True, vmem_limit_bytes=60 * 1024 * 1024
         ),
         name="conv_backward",
     )(activation, out_grad, weights, biases)

time: 55.8 us -> 44.4 us (0.80)
  Pallas kernels: 49.2 us -> 39.5 us
  local copies, waits for them, and re-layouts: 5.74 us -> 3.87 us
    pallas_call x1, Pallas kernels: 49.2 us -> 39.5 us  [fused(): pl.pallas_call(functools.partial(kernel, ranks), out_shape=(jax.ShapeDtyp...]
    unnamed x10 -> x4, local copies, waits for them, and re-layouts: 5.12 us -> 2.55 us
    slice x1, local copies, waits for them, and re-layouts: 0.63 us -> 1.32 us  [shards(): return (gin[None], wg, bg[:, 0])]
where the time goes in v2:
time: 44.4 us; the launch traced here: 44 us
  Pallas kernels  39.5 us (89%)
  local copies, waits for them, and re-layouts  3.87 us (9%)
  between operations  0.64 us (1%)
    pallas_call x1, Pallas kernels, fused(): pl.pallas_call(functools.partial(kernel, ranks), out_shape=(jax.ShapeDtyp...  39.5 us
    unnamed x4, local copies, waits for them, and re-layouts  2.55 us
    slice x1, local copies, waits for them, and re-layouts, shards(): return (gin[None], wg, bg[:, 0])  1.32 us

profile of v2, /device:TPU:1, one launch (start us, length us, event | category | flops | bytes accessed | tf_op | source)
XLA Modules:
  0.0 44.0 jit_solution(7655295069966738644)
XLA Ops:
  0.6 39.5 %conv_backward.1 = (bf16[16,8,2048]{2,1,0:T(8,128)(2,1)}, f32[9,16,128]{2,1,0:T(8,128)}, f32[16,128]{1,0:T(8,128)}) custom-call(bf16[16,8,2048]{2,1,0:T(8,128)(2,1)} %bitcast.4, bf16[16,8,2048]{2,1,0:T(8,128)(2,1)} %bitcast.5, bf16[9,128,128]{2,1,0:T(8,128)(2,1)} %w_ref.1, f32[1,128]{1,0:T(1,128)} %bitcast.7), custom_call_target="tpu_custom_call" | custom-call | tf_op jit(solution)/shard_map/conv_backward/pallas_call | solution.py:482
  40.1 1.3 %slice_reduce_fusion = f32[16]{0:T(128)} fusion(f32[16,128]{1,0:T(8,128)} %get-tuple-element.8), kind=kLoop, calls=%fused_computation | loop fusion | bytes 128 | tf_op jit(solution)/shard_map/slice | solution.py:546
  41.4 0.0 copy-start
  41.4 1.9 %copy.9 = bf16[1,16,8,2048]{3,2,1,0:T(8,128)(2,1)} copy(bf16[1,16,8,2048]{3,2,1,0:T(8,128)(2,1)} %bitcast.6) | data formatting | bytes 1048576
  43.4 0.0 copy-done
  43.4 0.6 %copy.10 = f32[9,16,128]{2,1,0:T(8,128)} copy(f32[9,16,128]{2,1,0:T(8,128)S(1)} %copy-done) | data formatting | bytes 147456
Async XLA Ops:
  41.4 1.9 %copy-start = (f32[9,16,128]{2,1,0:T(8,128)S(1)}, f32[9,16,128]{2,1,0:T(8,128)}, u32[]{:S(2)}) copy-start(f32[9,16,128]{2,1,0:T(8,128)} %get-tuple-element.13) | copy-start | bytes 221188

commit v3 on v2

--- a/solution.py
+++ b/solution.py
@@ -81,9 +81,8 @@
     og_ref,
     w_ref,
     bias_ref,
-    gin_ref,
-    wg_ref,
-    bg_ref,
+    gin_r,
+    part_r,
     act_v,
     og_v,
     perm,
@@ -99,16 +98,12 @@
     w_bwd,
     total,
     gin_s,
-    gin_r,
-    back,
-    out_v,
     wg_acc,
     b_acc,
     wg_s,
     wg_r,
     part,
-    part_r,
-    full,
+    ring_sem,
     load_sem,
     a2a_send,
     a2a_recv,
@@ -120,7 +115,6 @@
     wg_recv,
     part_send,
     part_recv,
-    out_sem,
 ):
     r = lax.axis_index("rows")
     c = lax.axis_index("chan")
@@ -161,39 +155,31 @@
         )
         return carry
 
-    def greet_rows(s, carry):
-        pl.semaphore_signal(
-            barrier, inc=1, device_id={"rows": lax.rem(r + s, ranks)}, device_id_type=MESH
-        )
-        return carry
-
     lax.fori_loop(1, PEERS, greet_chan, 0)
-    lax.fori_loop(1, ranks, greet_rows, 0)
-    border = ranks // 2 - 1 + far
-
-    @pl.when(r == border)
-    def _():
-        pl.semaphore_signal(
-            barrier,
-            inc=1,
-            device_id={"rows": ranks - 1 - border, "chan": flipped(c)},
-            device_id_type=MESH,
-        )
-
+
+    def ring_peer(step):
+        to = lax.rem(r + step + ranks, ranks)
+        its = to // (ranks // 2)
+        cross = far + its - 2 * far * its
+        return {"rows": to, "chan": c + cross * (flipped(c) - c)}
+
+    for step in (1, -1):
+        pl.semaphore_signal(barrier, inc=1, device_id=ring_peer(step), device_id_type=MESH)
+
+    def tell(n):
+        for step in (2**n, -(2**n))[: 1 if 2 ** (n + 1) == ranks else 2]:
+            pl.semaphore_signal(
+                ring_sem.at[n], inc=1, device_id=ring_peer(step), device_id_type=MESH
+            )
+
+    def hear(n):
+        pl.semaphore_wait(ring_sem.at[n], 1 if 2 ** (n + 1) == ranks else 2)
 
     perm[...] = column_phases()
     load_act.wait()
     split_phases(act_v, perm, tmp, act_s)
 
-    greeted = PEERS - 1 + ranks - 1
-
-    @pl.when(r == border)
-    def _():
-        pl.semaphore_wait(barrier, greeted + 1)
-
-    @pl.when(r != border)
-    def _():
-        pl.semaphore_wait(barrier, greeted)
+    pl.semaphore_wait(barrier, PEERS - 1 + 2)
 
     def exchange(kind, f, send, land, rows):
         def step(s, carry):
@@ -206,14 +192,9 @@
             send.at[f, slot_of(c)], land.at[f, rows, pl.ds(c16, OWN), :], a2a_recv.at[2 * kind + f]
         ).start()
 
-    def halo_peer(down):
-        to = lax.rem(r + (1 if down else ranks - 1), ranks)
-        cross = far + to // (ranks // 2) - 2 * far * (to // (ranks // 2))
-        return {"rows": to, "chan": c + cross * (flipped(c) - c)}
-
     def halo_copy(buf, kind, f, down):
         at = 2 * (2 * kind + f) + down
-        return remote(buf.at[f, 2 if down else 1], buf.at[f, 0 if down else 3], halo_send.at[at], halo_recv.at[at], halo_peer(down))
+        return remote(buf.at[f, 2 if down else 1], buf.at[f, 0 if down else 3], halo_send.at[at], halo_recv.at[at], ring_peer(1 if down else -1))
 
     def send_halos(buf, kind, f):
         @pl.when(r < ranks - 1)
@@ -245,6 +226,7 @@
     both = pl.ds(0, 2)
     exchange(0, 0, act_s, act_a, own)
     exchange(0, 1, act_s, act_a, own)
+    tell(0)
     load_og.wait()
     split_phases(og_v, perm, tmp, og_s)
     exchange(1, 0, og_s, og_a, both)
@@ -259,6 +241,8 @@
         jnp.int32, (CH, CH), 1
     )
     bias = jnp.sum(jnp.where(eye, bias_ref[...], 0.0), axis=1, keepdims=True)
+    hear(0)
+    tell(1)
     wg_acc[...] = jnp.zeros_like(wg_acc)
     b_acc[...] = jnp.zeros_like(b_acc)
 
@@ -281,9 +265,6 @@
             total[f, 0, :, cols] += dot(w[128 * up : 128 * up + 128, :], x[f, 0, :, cols])
             total[f, 1, :, cols] += dot(w[128 * down : 128 * down + 128, :], x[f, 3, :, cols])
 
-    out_w = pltpu.make_async_copy(full.at[pl.ds(0, 9)], wg_ref, out_sem.at[1])
-    out_b = pltpu.make_async_copy(full.at[9], bg_ref, out_sem.at[2])
-
     forward = (1, 0, 2)
     backward = (1, 2, 0)
 
@@ -390,56 +371,18 @@
         lax.fori_loop(1, ranks, step, 0)
         local(part, part_r.at[r], part_recv).start()
 
-    def finish_weight_grad():
-        wait_bytes(part_r, part_recv)
-        for t in range(PIECES):
-            x_of = min(t // HELD, xs - 1)
-            at = t - first_piece(x_of)
-            held = [
-                part_r[2 * (xs * half + x_of) + core, at].astype(F32)
-                for half in range(2)
-                for core in range(2)
-            ]
-            full[t] = (held[0] + held[1]) + (held[2] + held[3])
-        out_w.start()
-        out_b.start()
-
-    def join_phases(f):
-        wait_bytes(gin_r.at[f], ret_recv.at[f])
-        for b in range(4):
-            cols = slice(128 * b, 128 * (b + 1))
-            x = jnp.concatenate(
-                [
-                    jnp.concatenate([gin_r[f, 2 * phase + half, k, :, cols] for phase in range(4)], axis=1)
-                    for half in range(2)
-                    for k in range(2)
-                ],
-                axis=0,
-            )
-            y = lax.dot_general(x, perm[...], (((1,), (1,)), ((), ())), preferred_element_type=F32)
-            for half in range(2):
-                for k in range(2):
-                    h = 4 * k + 2 * half + f
-                    at = 16 * (2 * half + k)
-                    for n in range(4):
-                        back[4 * b + n, OWN * h : OWN * (h + 1), :] = y[
-                            at : at + 16, 128 * n : 128 * (n + 1)
-                        ]
-
-    def store_input_grad():
-        for n in range(16):
-            for ch in range(OWN):
-                rows = back[n, pl.ds(ch, 8, stride=OWN), :]
-                out_v[ch, :, 128 * n : 128 * (n + 1)] = rows.astype(BF16)
-        pltpu.make_async_copy(out_v, gin_ref, out_sem.at[0]).start()
-
     start_act(0)
+    hear(1)
+    tell(2)
     start_act(1)
+    hear(2)
+    tell(3)
     finish_pre(0)
     make_delta(0)
     finish_pre(1)
     add_weight_grad(0)
     start_input_grad(0)
+    hear(3)
     make_delta(1)
     add_weight_grad(1)
     send_weight_grad()
@@ -447,10 +390,9 @@
     start_input_grad(1)
     make_input_grad(1)
     send_parts()
-    join_phases(0)
-    join_phases(1)
-    store_input_grad()
-    finish_weight_grad()
+    for f in range(2):
+        wait_bytes(gin_r.at[f], ret_recv.at[f])
+    wait_bytes(part_r, part_recv)
 
     for f in range(2):
         wait_bytes(act_s.at[f, pl.ds(0, PEERS - 1)], a2a_send.at[f])
@@ -469,10 +411,6 @@
             def _():
                 halo_copy(buf, kind, f, 0).wait_send()
 
-    pltpu.make_async_copy(out_v, gin_ref, out_sem.at[0]).wait()
-    out_w.wait()
-    out_b.wait()
-
 
 def fused(ranks, activation, out_grad, weights, biases):
     height = activation.shape[1]
@@ -482,9 +420,8 @@
     return pl.pallas_call(
         functools.partial(kernel, ranks),
         out_shape=(
-            jax.ShapeDtypeStruct((OWN, height, extent), BF16),
-            jax.ShapeDtypeStruct((9, OWN, CH), F32),
-            jax.ShapeDtypeStruct((OWN, CH), F32),
+            vmem((2, PEERS, 2, OWN, COLS), BF16),
+            vmem((ranks, HELD, OWN, CH), BF16),
         ),
         in_specs=[
             pl.BlockSpec(memory_space=pl.ANY),
@@ -492,7 +429,7 @@
             pl.BlockSpec(memory_space=pl.ANY),
             pl.BlockSpec(memory_space=pltpu.VMEM),
         ],
-        out_specs=[pl.BlockSpec(memory_space=pl.ANY)] * 3,
+        out_specs=[pl.BlockSpec(memory_space=pl.ANY)] * 2,
         scratch_shapes=[
             vmem((OWN, height, extent), BF16),
             vmem((OWN, height, extent), BF16),
@@ -509,16 +446,12 @@
             vmem((3 * CH, 3 * CH), BF16),
             vmem((2, 2, CH, COLS), F32),
             vmem((2, 2, CH, COLS), BF16),
-            vmem((2, PEERS, 2, OWN, COLS), BF16),
-            vmem((16, CH, 128), F32),
-            vmem((OWN, height, extent), BF16),
             vmem((3, CH, 3 * CH), F32),
             vmem((CH, 1), F32),
             vmem((PEERS, PIECES, OWN, CH), BF16),
             vmem((ranks // 4 * PEERS, HELD, OWN, CH), BF16),
             vmem((HELD, OWN, CH), BF16),
-            vmem((ranks, HELD, OWN, CH), BF16),
-            vmem((PIECES, OWN, CH), F32),
+            pltpu.SemaphoreType.REGULAR((4,)),
             dma((3,)),
             dma((4,)),
             dma((4,)),
@@ -530,7 +463,6 @@
             dma,
             dma,
             dma,
-            dma((3,)),
         ],
         compiler_params=pltpu.CompilerParams(
             collective_id=0, has_side_effects=True, vmem_limit_bytes=60 * 1024 * 1024
@@ -539,11 +471,93 @@
     )(activation, out_grad, weights, biases)
 
 
+def outputs_kernel(
+    ranks, gin_v, part_v, gin_out, wg_out, bg_out, perm, back, out_v, full, sems
+):
+    perm[...] = column_phases()
+    stores = []
+    xs = ranks // 4
+    for t in range(PIECES):
+        x_of = min(t // HELD, xs - 1)
+        at = t - min(HELD * x_of, PIECES - HELD)
+        held = [
+            part_v[2 * (xs * half + x_of) + core, at].astype(F32)
+            for half in range(2)
+            for core in range(2)
+        ]
+        total = (held[0] + held[1]) + (held[2] + held[3])
+        if t < 9:
+            full[t] = total
+        else:
+            diagonal = lax.broadcasted_iota(jnp.int32, (OWN, CH), 0) == lax.broadcasted_iota(
+                jnp.int32, (OWN, CH), 1
+            )
+            bg_out[...] = jnp.sum(jnp.where(diagonal, total, 0.0), axis=0)[:OWN]
+    store = pltpu.make_async_copy(full, wg_out, sems.at[4])
+    store.start()
+    stores.append(store)
+    for b in range(4):
+        cols = slice(128 * b, 128 * (b + 1))
+        x = jnp.concatenate(
+            [
+                jnp.concatenate(
+                    [gin_v[h % 2, 2 * phase + (h % 4) // 2, h // 4, :, cols] for phase in range(4)],
+                    axis=1,
+                )
+                for h in range(8)
+            ],
+            axis=0,
+        )
+        y = lax.dot_general(x, perm[...], (((1,), (1,)), ((), ())), preferred_element_type=F32)
+        for n in range(4):
+            back[4 * b + n] = y[:, 128 * n : 128 * (n + 1)]
+        for n in range(4):
+            for ch in range(OWN):
+                rows = back[4 * b + n, pl.ds(ch, 8, stride=OWN), :]
+                at = COLS * b + 128 * n
+                out_v[ch, :, at : at + 128] = rows.astype(BF16)
+        part_of = pl.ds(COLS * b, COLS)
+        store = pltpu.make_async_copy(
+            out_v.at[:, :, part_of], gin_out.at[:, :, part_of], sems.at[b]
+        )
+        store.start()
+        stores.append(store)
+
+    for store in stores:
+        store.wait()
+
+
+def outputs(ranks, gin, parts, height, extent):
+    vmem = pltpu.VMEM
+    return pl.pallas_call(
+        functools.partial(outputs_kernel, ranks),
+        out_shape=(
+            jax.ShapeDtypeStruct((OWN, height, extent), BF16),
+            jax.ShapeDtypeStruct((9, OWN, CH), F32),
+            jax.ShapeDtypeStruct((OWN,), F32),
+        ),
+        in_specs=[pl.BlockSpec(memory_space=vmem)] * 2,
+        out_specs=(
+            pl.BlockSpec(memory_space=pl.ANY),
+            pl.BlockSpec(memory_space=pl.ANY),
+            pl.BlockSpec(memory_space=vmem),
+        ),
+        scratch_shapes=[
+            vmem((COLS, COLS), BF16),
+            vmem((16, CH, 128), F32),
+            vmem((OWN, height, extent), BF16),
+            vmem((9, OWN, CH), F32),
+            pltpu.SemaphoreType.DMA((5,)),
+        ],
+        compiler_params=pltpu.CompilerParams(vmem_limit_bytes=16 * 1024 * 1024),
+        name="conv_outputs",
+    )(gin, parts)
+
+
 def shards(ranks, activation, out_grad, weights, biases):
-    gin, wg, bg = fused(
-        ranks, activation[0], out_grad[0], weights, biases.reshape(1, CH)
-    )
-    return gin[None], wg, bg[:, 0]
+    gin, parts = fused(ranks, activation[0], out_grad[0], weights, biases.reshape(1, CH))
+    gin, wg, bg = outputs(ranks, gin, parts, activation.shape[2], activation.shape[3])
+    return gin[None], wg, bg
 
 
 def solution(mesh):

time: 44.4 us -> 41.5 us (0.935)
  local copies, waits for them, and re-layouts: 3.87 us -> 0 us
  Pallas kernels: 39.5 us -> 40.7 us
    unnamed x4 -> x0, local copies, waits for them, and re-layouts: 2.55 us -> none
    slice x1 -> x0, local copies, waits for them, and re-layouts: 1.32 us -> none  [shards(): return (gin[None], wg, bg[:, 0])]
    pallas_call x1 -> x2, Pallas kernels: 39.5 us -> 40.7 us  [the longest x1 38.5 us: fused(): pl.pallas_call(functools.partial(kernel, ranks), out_shape=(vmem((2, PEER...]
where the time goes in v3:
time: 41.5 us; the launch traced here: 41.4 us
  Pallas kernels  40.7 us (98%)
  between operations  0.64 us (2%)
    pallas_call x1, Pallas kernels, fused(): pl.pallas_call(functools.partial(kernel, ranks), out_shape=(vmem((2, PEER...  38.5 us
    pallas_call x1, Pallas kernels, outputs(): pl.pallas_call(functools.partial(outputs_kernel, ranks), out_shape=(jax.S...  2.25 us

profile of v3, /device:TPU:1, one launch (start us, length us, event | category | flops | bytes accessed | tf_op | source)
XLA Modules:
  0.0 41.4 jit_solution(117808947503012295)
XLA Ops:
  0.6 38.5 %conv_backward.1 = (bf16[2,8,2,16,512]{4,3,2,1,0:T(8,128)(2,1)S(1)}, bf16[16,3,16,128]{3,2,1,0:T(8,128)(2,1)S(1)}) custom-call(bf16[16,8,2048]{2,1,0:T(8,128)(2,1)} %bitcast.4, bf16[16,8,2048]{2,1,0:T(8,128)(2,1)} %bitcast.5, bf16[9,128,128]{2,1,0:T(8,128)(2,1)} %w_ref.1, f32[1,128]{1,0:T(1,128)} %bitcast.6), custom_call_target="tpu_custom_call" | custom-call | tf_op jit(solution)/shard_map/conv_backward/pallas_call | solution.py:420
  39.1 2.2 %conv_outputs.1 = (bf16[16,8,2048]{2,1,0:T(8,128)(2,1)}, f32[9,16,128]{2,1,0:T(8,128)}, f32[16]{0:T(128)}) custom-call(bf16[2,8,2,16,512]{4,3,2,1,0:T(8,128)(2,1)S(1)} %get-tuple-element.8.gin_v, bf16[16,3,16,128]{3,2,1,0:T(8,128)(2,1)S(1)} %get-tuple-element.9.part_v), custom_call_target="tpu_custom_call" | custom-call | tf_op jit(solution)/shard_map/conv_outputs/pallas_call | solution.py:532

commit v4 on v3

v4 whole, which is shorter than its diff:
```python
import functools

import jax
import jax.numpy as jnp
from jax import lax
from jax.experimental import pallas as pl
from jax.experimental.pallas import tpu as pltpu
from jax.sharding import PartitionSpec as P

MESH = pl.DeviceIdType.MESH
F32 = jnp.float32
BF16 = jnp.bfloat16

CH = 128
OWN = 16
PEERS = 8
COLS = 512
CHAN_STEPS = [(2, 1), (1, 1), (3, 1), (2, 0), (1, 0), (3, 0), (0, 1)]
ROW_STEPS = [(a, b, e) for a in (1, 0) for b in (2, 1, 3, 0) for e in (1, 0)][:-1]
SHARES = 4


def wait_bytes(ref, sem):
    pltpu.make_async_copy(ref, ref, sem).wait()


def remote(src, dst, send_sem, recv_sem, device):
    return pltpu.make_async_remote_copy(
        src_ref=src,
        dst_ref=dst,
        send_sem=send_sem,
        recv_sem=recv_sem,
        device_id=device,
        device_id_type=MESH,
    )


def local(src, dst, sem):
    return pltpu.make_async_copy(src, dst, sem)


def column_phases():
    w = lax.broadcasted_iota(jnp.int32, (COLS, COLS), 0)
    m = lax.broadcasted_iota(jnp.int32, (COLS, COLS), 1)
    return jnp.where(w == 4 * (m & 127) + (m >> 7), 1.0, 0.0).astype(BF16)


def split_phases(b, block, perm, tmp, send):
    x = block[:, :, COLS * b : COLS * (b + 1)].astype(F32).reshape(CH, COLS).astype(BF16)
    y = jnp.dot(x, perm[...], preferred_element_type=F32)
    for phase in range(4):
        tmp[4 * b + phase] = y[:, 128 * phase : 128 * (phase + 1)]
    for phase in range(4):
        for h in range(8):
            f, half, k = h % 2, (h % 4) // 2, h // 4
            rows = tmp[4 * b + phase, pl.ds(h, OWN, stride=8), :]
            send[f, 2 * phase + half, k, :, 128 * b : 128 * (b + 1)] = rows.astype(BF16)


def stack_shifts(src, dst, ahead):
    def body(i, carry):
        at = pl.multiple_of(i * 32, 32)
        x = src[pl.ds(at, 32), :]
        lane = lax.broadcasted_iota(jnp.int32, (32, COLS), 1)
        xf = x.astype(F32)
        later = jnp.where(lane == 0, 0.0, pltpu.roll(xf, 1, 1)).astype(BF16)
        earlier = jnp.where(lane == COLS - 1, 0.0, pltpu.roll(xf, COLS - 1, 1)).astype(BF16)
        first, last = (earlier, later) if ahead else (later, earlier)
        dst[pl.ds(at, 32), :] = first
        dst[pl.ds(at + 128, 32), :] = x
        dst[pl.ds(at + 256, 32), :] = last
        return carry

    lax.fori_loop(0, CH // 32, body, 0, unroll=True)


def kernel(
    ranks,
    act_ref,
    og_ref,
    w_ref,
    bias_ref,
    gin_out,
    part_r,
    act_v,
    og_v,
    bias_v,
    perm,
    tmp,
    act_s,
    og_s,
    act_a,
    og_a,
    act_x,
    delta_a,
    delta_x,
    w_fwd,
    w_bwd,
    total,
    gin_s,
    gin_r,
    back,
    wg_acc,
    b_acc,
    wg_s,
    wg_r,
    b_s,
    b_r,
    part,
    ring_sem,
    load_sem,
    a2a_send,
    a2a_recv,
    halo_send,
    halo_recv,
    ret_send,
    ret_recv,
    wg_send,
    wg_recv,
    b_send,
    b_recv,
    part_send,
    part_recv,
):
    r = lax.axis_index("rows")
    c = lax.axis_index("chan")
    c16 = pl.multiple_of(c * OWN, OWN)
    far = r // (ranks // 2)

    xs = ranks // 4
    x = lax.rem(r // 2, xs)

    def flipped(at):
        return at + 1 - 2 * lax.rem(at, 2)

    def slot_of(at):
        return at + far * (flipped(at) - at)

    dot = functools.partial(jnp.dot, preferred_element_type=F32)

    barrier = pltpu.get_barrier_semaphore()

    def chan_peer(dz, dy):
        return 2 * lax.rem(c // 2 + dz, PEERS // 2) + lax.rem(c + dy, 2)

    chan_peers = [chan_peer(*step) for step in CHAN_STEPS]
    for to in chan_peers:
        pl.semaphore_signal(barrier, inc=1, device_id={"chan": to}, device_id_type=MESH)

    def ring_peer(step):
        to = lax.rem(r + step + ranks, ranks)
        its = to // (ranks // 2)
        cross = far + its - 2 * far * its
        return {"rows": to, "chan": c + cross * (flipped(c) - c)}

    for step in (1, -1):
        pl.semaphore_signal(barrier, inc=1, device_id=ring_peer(step), device_id_type=MESH)

    loads_act = [
        pltpu.make_async_copy(
            act_ref.at[:, :, pl.ds(COLS * b, COLS)],
            act_v.at[:, :, pl.ds(COLS * b, COLS)],
            load_sem.at[b],
        )
        for b in range(4)
    ]
    for load in loads_act:
        load.start()
    load_og = pltpu.make_async_copy(og_ref, og_v, load_sem.at[4])
    load_og.start()

    def tell(n):
        for step in (2**n, -(2**n))[: 1 if 2 ** (n + 1) == ranks else 2]:
            pl.semaphore_signal(
                ring_sem.at[n], inc=1, device_id=ring_peer(step), device_id_type=MESH
            )

    def hear(n):
        pl.semaphore_wait(ring_sem.at[n], 1 if 2 ** (n + 1) == ranks else 2)

    perm[...] = column_phases()
    for b in range(4):
        loads_act[b].wait()
        split_phases(b, act_v, perm, tmp, act_s)

    pl.semaphore_wait(barrier, PEERS - 1 + 2)

    def exchange(kind, f, send, land, rows):
        for to in chan_peers:
            remote(
                send.at[f, slot_of(to)],
                land.at[f, rows, pl.ds(c16, OWN), :],
                a2a_send.at[2 * kind + f],
                a2a_recv.at[2 * kind + f],
                {"chan": to},
            ).start()
        local(
            send.at[f, slot_of(c)], land.at[f, rows, pl.ds(c16, OWN), :], a2a_recv.at[2 * kind + f]
        ).start()

    def halo_copy(buf, kind, f, down):
        at = 2 * (2 * kind + f) + down
        return remote(buf.at[f, 2 if down else 1], buf.at[f, 0 if down else 3], halo_send.at[at], halo_recv.at[at], ring_peer(1 if down else -1))

    def send_halos(buf, kind, f):
        @pl.when(r < ranks - 1)
        def _():
            halo_copy(buf, kind, f, 1).start()

        @pl.when(r > 0)
        def _():
            halo_copy(buf, kind, f, 0).start()

    def wait_halos(buf, kind, f):
        @pl.when(r > 0)
        def _():
            halo_copy(buf, kind, f, 1).wait_recv()

        @pl.when(r == 0)
        def _():
            buf[f, 0] = jnp.zeros((CH, COLS), BF16)

        @pl.when(r < ranks - 1)
        def _():
            halo_copy(buf, kind, f, 0).wait_recv()

        @pl.when(r == ranks - 1)
        def _():
            buf[f, 3] = jnp.zeros((CH, COLS), BF16)

    own = pl.ds(1, 2)
    both = pl.ds(0, 2)
    exchange(0, 0, act_s, act_a, own)
    exchange(0, 1, act_s, act_a, own)
    for p in range(3):
        for q in range(3):
            pltpu.make_async_copy(
                w_ref.at[3 * p + q],
                w_fwd.at[pl.ds(128 * p, 128), pl.ds(128 * q, 128)],
                load_sem.at[5],
            ).start()
    load_bias = pltpu.make_async_copy(bias_ref, bias_v, load_sem.at[6])
    load_bias.start()
    tell(0)
    load_og.wait()
    for b in range(4):
        split_phases(b, og_v, perm, tmp, og_s)
    exchange(1, 0, og_s, og_a, both)
    exchange(1, 1, og_s, og_a, both)

    pltpu.make_async_copy(w_fwd, w_fwd, load_sem.at[5]).wait()
    load_bias.wait()
    for p in range(3):
        for q in range(3):
            at = (pl.ds(128 * p, 128), pl.ds(128 * q, 128))
            w_bwd[at] = w_fwd[at].astype(F32).T.astype(BF16)
    eye = lax.broadcasted_iota(jnp.int32, (CH, CH), 0) == lax.broadcasted_iota(
        jnp.int32, (CH, CH), 1
    )
    bias = jnp.sum(jnp.where(eye, bias_v[...], 0.0), axis=1, keepdims=True)
    hear(0)
    tell(1)
    b_acc[...] = jnp.zeros_like(b_acc)

    def taps_own(w, x, f, order):
        keep, up, down = order
        for n in range(2):
            cols = pl.ds(256 * n, 256)
            first = x[f, 1, :, cols]
            second = x[f, 2, :, cols]
            w_keep = w[128 * keep : 128 * keep + 128, :]
            w_up = w[128 * up : 128 * up + 128, :]
            w_down = w[128 * down : 128 * down + 128, :]
            total[f, 0, :, cols] = dot(w_keep, first) + dot(w_down, second)
            total[f, 1, :, cols] = dot(w_up, first) + dot(w_keep, second)

    def taps_halo(w, x, f, order):
        keep, up, down = order
        for n in range(2):
            cols = pl.ds(256 * n, 256)
            total[f, 0, :, cols] += dot(w[128 * up : 128 * up + 128, :], x[f, 0, :, cols])
            total[f, 1, :, cols] += dot(w[128 * down : 128 * down + 128, :], x[f, 3, :, cols])

    forward = (1, 0, 2)
    backward = (1, 2, 0)

    def start_act(f):
        wait_bytes(act_a.at[f, own], a2a_recv.at[f])
        send_halos(act_a, 0, f)
        for k in (1, 2):
            stack_shifts(act_a.at[f, k], act_x.at[f, k], False)

        taps_own(w_fwd, act_x, f, forward)

    def finish_pre(f):
        wait_halos(act_a, 0, f)
        for k in (0, 3):
            stack_shifts(act_a.at[f, k], act_x.at[f, k], False)
        taps_halo(w_fwd, act_x, f, forward)

    def make_delta(f):
        wait_bytes(og_a.at[f], a2a_recv.at[2 + f])
        for k in range(2):
            for at in range(0, CH, 16):
                rows = slice(at, at + 16)
                pre = total[f, k, rows, :] + bias[rows, :]
                s = jax.nn.sigmoid(pre)
                delta = (og_a[f, k, rows, :].astype(F32) * s * (1.0 + pre * (1.0 - s))).astype(BF16)
                delta_a[f, 1 + k, rows, :] = delta
                b_acc[rows, :] += jnp.sum(delta.astype(F32), axis=1, keepdims=True)
        send_halos(delta_a, 1, f)

    def tap_row_grad(p, f):
        grads = [
            lax.dot_general(
                delta_a[f, 1 + k],
                act_x[f, k + p],
                (((1,), (1,)), ((), ())),
                preferred_element_type=F32,
            )
            for k in range(2)
        ]
        return grads[0] + grads[1]

    def add_weight_grad(f):
        for p in range(3):
            wg_acc[p] = tap_row_grad(p, f)

    def start_input_grad(f):
        for k in (1, 2):
            stack_shifts(delta_a.at[f, k], delta_x.at[f, k], True)
        taps_own(w_bwd, delta_x, f, backward)

    def make_input_grad(f):
        wait_halos(delta_a, 1, f)
        for k in (0, 3):
            stack_shifts(delta_a.at[f, k], delta_x.at[f, k], True)
        taps_halo(w_bwd, delta_x, f, backward)
        for k in range(2):
            gin_s[f, k] = total[f, k].astype(BF16)

        for to in chan_peers:
            remote(
                gin_s.at[f, :, pl.ds(pl.multiple_of(to * OWN, OWN), OWN), :],
                gin_r.at[f, slot_of(c)],
                ret_send.at[f],
                ret_recv.at[f],
                {"chan": to},
            ).start()
        local(
            gin_s.at[f, :, pl.ds(c16, OWN), :], gin_r.at[f, slot_of(c)], ret_recv.at[f]
        ).start()

    sender = x * PEERS + c

    def send_shares(at, send, land, send_sem, recv_sem):
        def share_copy(to):
            return remote(
                send.at[to],
                land.at[sender],
                send_sem,
                recv_sem,
                {"rows": r + 2 * (at - x), "chan": to},
            )

        for to in chan_peers:
            share_copy(to).start()

        @pl.when(x != at)
        def _():
            share_copy(c).start()

        @pl.when(x == at)
        def _():
            local(send.at[c], land.at[sender], recv_sem).start()

    def send_weight_grad(f):
        for d in range(PEERS):
            rows = slice(OWN * d, OWN * (d + 1))
            b_s[d] = jnp.broadcast_to(b_acc[rows, :], (OWN, CH)).astype(BF16)
        for dx in (2, 1, 3, 0):
            p = lax.rem(x + dx, xs)

            @pl.when(p == 3)
            def _():
                send_shares(p, b_s, b_r, b_send, b_recv)

            @pl.when(p < 3)
            def _():
                grad = (wg_acc[p] + tap_row_grad(p, f)).astype(BF16)
                for d in range(PEERS):
                    for q in range(3):
                        wg_s[p, d, q] = grad[OWN * d : OWN * (d + 1), 128 * q : 128 * (q + 1)]
                send_shares(p, wg_s.at[p], wg_r, wg_send, wg_recv)

    share = 2 * far + lax.rem(r, 2)

    def send_part(src, land):
        for dfar, dx, dcore in ROW_STEPS:
            to = 2 * (xs * lax.rem(far + dfar, 2) + lax.rem(x + dx, xs)) + lax.rem(r + dcore, 2)
            remote(src, land, part_send, part_recv, {"rows": to}).start()
        local(src, land, part_recv).start()

    def send_parts():
        @pl.when(x < 3)
        def _():
            wait_bytes(wg_r, wg_recv)
            for q in range(3):
                acc = wg_r[0, q].astype(F32)
                for d in range(1, xs * PEERS):
                    acc += wg_r[d, q].astype(F32)
                part[q] = acc.astype(BF16)
            send_part(part, part_r.at[pl.ds((x * SHARES + share) * 3, 3)])

        @pl.when(x == 3)
        def _():
            wait_bytes(b_r, b_recv)
            acc = b_r[0].astype(F32)
            for d in range(1, xs * PEERS):
                acc += b_r[d].astype(F32)
            part[0] = acc.astype(BF16)
            send_part(part.at[pl.ds(0, 1)], part_r.at[pl.ds(9 * SHARES + share, 1)])

    def wait_parts_sent():
        @pl.when(x < 3)
        def _():
            wait_bytes(wg_r.at[pl.ds(0, 3 * PEERS - 1)], wg_send)
            wait_bytes(b_r.at[pl.ds(0, PEERS)], b_send)
            wait_bytes(wg_r.at[pl.ds(0, ranks - 1)], part_send)

        @pl.when(x == 3)
        def _():
            wait_bytes(wg_r.at[pl.ds(0, 3 * PEERS)], wg_send)
            wait_bytes(b_r.at[pl.ds(0, PEERS - 1)], b_send)
            wait_bytes(b_r.at[pl.ds(0, ranks - 1)], part_send)

    def join_phases(f):
        wait_bytes(gin_r.at[f], ret_recv.at[f])
        for b in range(4):
            cols = slice(128 * b, 128 * (b + 1))
            x = jnp.concatenate(
                [
                    jnp.concatenate([gin_r[f, 2 * phase + half, k, :, cols] for phase in range(4)], axis=1)
                    for k in range(2)
                    for half in range(2)
                ],
                axis=0,
            )
            y = lax.dot_general(x, perm[...], (((1,), (1,)), ((), ())), preferred_element_type=F32)
            for i in range(4):
                h = 2 * i + f
                for n in range(4):
                    back[4 * b + n, OWN * h : OWN * (h + 1), :] = y[
                        OWN * i : OWN * (i + 1), 128 * n : 128 * (n + 1)
                    ]

    def store_input_grad():
        for n in range(16):
            for ch in range(OWN):
                rows = back[n, pl.ds(ch, 8, stride=OWN), :]
                gin_out[ch, :, 128 * n : 128 * (n + 1)] = rows.astype(BF16)

    start_act(0)
    hear(1)
    tell(2)
    start_act(1)
    hear(2)
    tell(3)
    finish_pre(0)
    make_delta(0)
    finish_pre(1)
    add_weight_grad(0)
    start_input_grad(0)
    hear(3)
    make_delta(1)
    send_weight_grad(1)
    make_input_grad(0)
    start_input_grad(1)
    make_input_grad(1)
    send_parts()
    join_phases(0)
    join_phases(1)
    store_input_grad()
    wait_bytes(part_r, part_recv)

    for f in range(2):
        wait_bytes(act_s.at[f, pl.ds(0, PEERS - 1)], a2a_send.at[f])
        wait_bytes(og_s.at[f, pl.ds(0, PEERS - 1)], a2a_send.at[2 + f])
        wait_bytes(gin_r.at[f, pl.ds(0, PEERS - 1)], ret_send.at[f])
    wait_parts_sent()
    for kind, buf in ((0, act_a), (1, delta_a)):
        for f in range(2):

            @pl.when(r < ranks - 1)
            def _():
                halo_copy(buf, kind, f, 1).wait_send()

            @pl.when(r > 0)
            def _():
                halo_copy(buf, kind, f, 0).wait_send()


def fused(ranks, activation, out_grad, weights, biases):
    height = activation.shape[1]
    extent = activation.shape[2]
    vmem = pltpu.VMEM
    dma = pltpu.SemaphoreType.DMA
    return pl.pallas_call(
        functools.partial(kernel, ranks),
        out_shape=(
            vmem((OWN, height, extent), BF16),
            vmem((10 * SHARES, OWN, CH), BF16),
        ),
        in_specs=[
            pl.BlockSpec(memory_space=pl.ANY),
            pl.BlockSpec(memory_space=pl.ANY),
            pl.BlockSpec(memory_space=pl.ANY),
            pl.BlockSpec(memory_space=pl.ANY),
        ],
        out_specs=[
            pl.BlockSpec(memory_space=pltpu.VMEM),
            pl.BlockSpec(memory_space=pl.ANY),
        ],
        scratch_shapes=[
            vmem((OWN, height, extent), BF16),
            vmem((OWN, height, extent), BF16),
            vmem((1, CH), F32),
            vmem((COLS, COLS), BF16),
            vmem((16, CH, 128), F32),
            vmem((2, PEERS, 2, OWN, COLS), BF16),
            vmem((2, PEERS, 2, OWN, COLS), BF16),
            vmem((2, 4, CH, COLS), BF16),
            vmem((2, 2, CH, COLS), BF16),
            vmem((2, 4, 3 * CH, COLS), BF16),
            vmem((2, 4, CH, COLS), BF16),
            vmem((2, 4, 3 * CH, COLS), BF16),
            vmem((3 * CH, 3 * CH), BF16),
            vmem((3 * CH, 3 * CH), BF16),
            vmem((2, 2, CH, COLS), F32),
            vmem((2, 2, CH, COLS), BF16),
            vmem((2, PEERS, 2, OWN, COLS), BF16),
            vmem((16, CH, 128), F32),
            vmem((3, CH, 3 * CH), F32),
            vmem((CH, 1), F32),
            vmem((3, PEERS, 3, OWN, CH), BF16),
            vmem((4 * PEERS, 3, OWN, CH), BF16),
            vmem((PEERS, OWN, CH), BF16),
            vmem((4 * PEERS, OWN, CH), BF16),
            vmem((3, OWN, CH), BF16),
            pltpu.SemaphoreType.REGULAR((4,)),
            dma((7,)),
            dma((4,)),
            dma((4,)),
            dma((8,)),
            dma((8,)),
            dma((2,)),
            dma((2,)),
            dma,
            dma,
            dma,
            dma,
            dma,
            dma,
        ],
        compiler_params=pltpu.CompilerParams(
            collective_id=0, has_side_effects=True, vmem_limit_bytes=60 * 1024 * 1024
        ),
        name="conv_backward",
    )(activation, out_grad, weights, biases)


def outputs_kernel(gin_ref, part_ref, gin_out, wg_out, bg_out, full, bg_v, sems):
    stores = [pltpu.make_async_copy(gin_ref, gin_out, sems.at[0])]
    stores[0].start()

    def total(shares):
        held = [part_ref[at].astype(F32) for at in shares]
        return (held[0] + held[1]) + (held[2] + held[3])

    for p in range(3):
        for q in range(3):
            full[3 * p + q] = total([(p * SHARES + i) * 3 + q for i in range(SHARES)])
    stores.append(pltpu.make_async_copy(full, wg_out, sems.at[1]))
    stores[1].start()
    diagonal = lax.broadcasted_iota(jnp.int32, (OWN, CH), 0) == lax.broadcasted_iota(
        jnp.int32, (OWN, CH), 1
    )
    bias = total([9 * SHARES + i for i in range(SHARES)])
    bg_v[...] = jnp.sum(jnp.where(diagonal, bias, 0.0), axis=0)[:OWN]
    stores.append(pltpu.make_async_copy(bg_v, bg_out, sems.at[2]))
    stores[2].start()
    for store in stores:
        store.wait()


def outputs(gin, parts):
    vmem = pltpu.VMEM
    return pl.pallas_call(
        outputs_kernel,
        out_shape=(
            jax.ShapeDtypeStruct(gin.shape, BF16),
            jax.ShapeDtypeStruct((9, OWN, CH), F32),
            jax.ShapeDtypeStruct((OWN,), F32),
        ),
        in_specs=[pl.BlockSpec(memory_space=vmem)] * 2,
        out_specs=(
            pl.BlockSpec(memory_space=pl.ANY),
            pl.BlockSpec(memory_space=pl.ANY),
            pl.BlockSpec(memory_space=pl.ANY),
        ),
        scratch_shapes=[vmem((9, OWN, CH), F32), vmem((OWN,), F32), pltpu.SemaphoreType.DMA((3,))],
        compiler_params=pltpu.CompilerParams(vmem_limit_bytes=16 * 1024 * 1024),
        name="conv_outputs",
    )(gin, parts)


def shards(ranks, activation, out_grad, weights, biases):
    gin, parts = fused(ranks, activation[0], out_grad[0], weights, biases.reshape(1, CH))
    gin, wg, bg = outputs(gin, parts)
    return gin[None], wg, bg


def solution(mesh):
    return jax.shard_map(
        functools.partial(shards, mesh.shape["rows"]),
        mesh=mesh,
        in_specs=(P(None, "chan", "rows", None), P(None, "chan", "rows", None), P(), P()),
        out_specs=(P(None, "chan", "rows", None), P(None, "chan", None), P("chan")),
        check_vma=False,
    )
```

time: 41.5 us -> 39.4 us (0.949)
  Pallas kernels: 40.7 us -> 38.6 us
    pallas_call x2, Pallas kernels: 40.7 us -> 38.6 us  [the longest x1 37.7 us: fused(): pl.pallas_call(functools.partial(kernel, ranks), out_shape=(vmem((OWN, he...]
where the time goes in v4:
time: 39.4 us; the launch traced here: 39.2 us
  Pallas kernels  38.6 us (98%)
  between operations  0.64 us (2%)
    pallas_call x1, Pallas kernels, fused(): pl.pallas_call(functools.partial(kernel, ranks), out_shape=(vmem((OWN, he...  37.7 us
    pallas_call x1, Pallas kernels, outputs(): pl.pallas_call(outputs_kernel, out_shape=(jax.ShapeDtypeStruct(gin.shape,...  0.84 us

profile of v4, /device:TPU:1, one launch (start us, length us, event | category | flops | bytes accessed | tf_op | source)
XLA Modules:
  0.0 39.2 jit_solution(6287479765063977098)
XLA Ops:
  0.6 37.7 %conv_backward.1 = (bf16[16,8,2048]{2,1,0:T(8,128)(2,1)S(1)}, bf16[40,16,128]{2,1,0:T(8,128)(2,1)S(1)}) custom-call(bf16[16,8,2048]{2,1,0:T(8,128)(2,1)} %bitcast.4, bf16[16,8,2048]{2,1,0:T(8,128)(2,1)} %bitcast.5, bf16[9,128,128]{2,1,0:T(8,128)(2,1)} %w_ref.1, f32[1,128]{1,0:T(1,128)} %bitcast.6), custom_call_target="tpu_custom_call" | custom-call | tf_op jit(solution)/shard_map/conv_backward/pallas_call | solution.py:508
  38.4 0.8 %conv_outputs.1 = (bf16[16,8,2048]{2,1,0:T(8,128)(2,1)}, f32[9,16,128]{2,1,0:T(8,128)}, f32[16]{0:T(128)}) custom-call(bf16[16,8,2048]{2,1,0:T(8,128)(2,1)S(1)} %get-tuple-element.8.gin_ref, bf16[40,16,128]{2,1,0:T(8,128)(2,1)S(1)} %get-tuple-element.9.part_ref), custom_call_target="tpu_custom_call" | custom-call | tf_op jit(solution)/shard_map/conv_outputs/pallas_call | solution.py:598

commit v5 on v4

--- a/solution.py
+++ b/solution.py
@@ -17,7 +17,7 @@
 COLS = 512
 CHAN_STEPS = [(2, 1), (1, 1), (3, 1), (2, 0), (1, 0), (3, 0), (0, 1)]
 ROW_STEPS = [(a, b, e) for a in (1, 0) for b in (2, 1, 3, 0) for e in (1, 0)][:-1]
-SHARES = 4
+SHARES = 2
 
 
 def wait_bytes(ref, sem):
@@ -104,8 +104,12 @@
     b_acc,
     wg_s,
     wg_r,
+    wg_c,
+    wg_t,
     b_s,
     b_r,
+    b_c,
+    b_t,
     part,
     ring_sem,
     load_sem,
@@ -119,6 +123,8 @@
     wg_recv,
     b_send,
     b_recv,
+    core_send,
+    core_recv,
     part_send,
     part_recv,
 ):
@@ -185,17 +191,17 @@
 
     pl.semaphore_wait(barrier, PEERS - 1 + 2)
 
-    def exchange(kind, f, send, land, rows):
+    def exchange(at, f, send, land, from_k, to_k):
         for to in chan_peers:
             remote(
-                send.at[f, slot_of(to)],
-                land.at[f, rows, pl.ds(c16, OWN), :],
-                a2a_send.at[2 * kind + f],
-                a2a_recv.at[2 * kind + f],
+                send.at[f, slot_of(to), from_k],
+                land.at[f, to_k, pl.ds(c16, OWN), :],
+                a2a_send.at[at],
+                a2a_recv.at[at],
                 {"chan": to},
             ).start()
         local(
-            send.at[f, slot_of(c)], land.at[f, rows, pl.ds(c16, OWN), :], a2a_recv.at[2 * kind + f]
+            send.at[f, slot_of(c), from_k], land.at[f, to_k, pl.ds(c16, OWN), :], a2a_recv.at[at]
         ).start()
 
     def halo_copy(buf, kind, f, down):
@@ -230,8 +236,8 @@
 
     own = pl.ds(1, 2)
     both = pl.ds(0, 2)
-    exchange(0, 0, act_s, act_a, own)
-    exchange(0, 1, act_s, act_a, own)
+    exchange(0, 0, act_s, act_a, both, own)
+    exchange(1, 1, act_s, act_a, both, own)
     for p in range(3):
         for q in range(3):
             pltpu.make_async_copy(
@@ -245,8 +251,9 @@
     load_og.wait()
     for b in range(4):
         split_phases(b, og_v, perm, tmp, og_s)
-    exchange(1, 0, og_s, og_a, both)
-    exchange(1, 1, og_s, og_a, both)
+    exchange(2, 0, og_s, og_a, both, both)
+    for k in range(2):
+        exchange(3 + k, 1, og_s, og_a, pl.ds(k, 1), pl.ds(k, 1))
 
     pltpu.make_async_copy(w_fwd, w_fwd, load_sem.at[5]).wait()
     load_bias.wait()
@@ -298,9 +305,8 @@
             stack_shifts(act_a.at[f, k], act_x.at[f, k], False)
         taps_halo(w_fwd, act_x, f, forward)
 
-    def make_delta(f):
-        wait_bytes(og_a.at[f], a2a_recv.at[2 + f])
-        for k in range(2):
+    def make_delta(f, ks):
+        for k in ks:
             for at in range(0, CH, 16):
                 rows = slice(at, at + 16)
                 pre = total[f, k, rows, :] + bias[rows, :]
@@ -308,23 +314,14 @@
                 delta = (og_a[f, k, rows, :].astype(F32) * s * (1.0 + pre * (1.0 - s))).astype(BF16)
                 delta_a[f, 1 + k, rows, :] = delta
                 b_acc[rows, :] += jnp.sum(delta.astype(F32), axis=1, keepdims=True)
-        send_halos(delta_a, 1, f)
-
-    def tap_row_grad(p, f):
-        grads = [
-            lax.dot_general(
-                delta_a[f, 1 + k],
-                act_x[f, k + p],
-                (((1,), (1,)), ((), ())),
-                preferred_element_type=F32,
-            )
-            for k in range(2)
-        ]
-        return grads[0] + grads[1]
-
-    def add_weight_grad(f):
-        for p in range(3):
-            wg_acc[p] = tap_row_grad(p, f)
+
+    def tap_row_grad(p, f, k):
+        return lax.dot_general(
+            delta_a[f, 1 + k],
+            act_x[f, k + p],
+            (((1,), (1,)), ((), ())),
+            preferred_element_type=F32,
+        )
 
     def start_input_grad(f):
         for k in (1, 2):
@@ -339,61 +336,78 @@
         for k in range(2):
             gin_s[f, k] = total[f, k].astype(BF16)
 
+    def return_input_grad(f, k):
         for to in chan_peers:
             remote(
-                gin_s.at[f, :, pl.ds(pl.multiple_of(to * OWN, OWN), OWN), :],
-                gin_r.at[f, slot_of(c)],
+                gin_s.at[f, k, pl.ds(pl.multiple_of(to * OWN, OWN), OWN), :],
+                gin_r.at[f, slot_of(c), k],
                 ret_send.at[f],
                 ret_recv.at[f],
                 {"chan": to},
             ).start()
         local(
-            gin_s.at[f, :, pl.ds(c16, OWN), :], gin_r.at[f, slot_of(c)], ret_recv.at[f]
+            gin_s.at[f, k, pl.ds(c16, OWN), :], gin_r.at[f, slot_of(c), k], ret_recv.at[f]
         ).start()
 
+    core = lax.rem(r, 2)
+    owner = c // 4 == core
     sender = x * PEERS + c
-
-    def send_shares(at, send, land, send_sem, recv_sem):
-        def share_copy(to):
-            return remote(
-                send.at[to],
-                land.at[sender],
-                send_sem,
-                recv_sem,
-                {"rows": r + 2 * (at - x), "chan": to},
-            )
-
-        for to in chan_peers:
-            share_copy(to).start()
-
-        @pl.when(x != at)
-        def _():
-            share_copy(c).start()
-
-        @pl.when(x == at)
-        def _():
-            local(send.at[c], land.at[sender], recv_sem).start()
-
-    def send_weight_grad(f):
-        for d in range(PEERS):
-            rows = slice(OWN * d, OWN * (d + 1))
-            b_s[d] = jnp.broadcast_to(b_acc[rows, :], (OWN, CH)).astype(BF16)
+    other_core = {"rows": r + 1 - 2 * core}
+
+    def block_rows(of, j):
+        return pl.ds(pl.multiple_of(64 * of + OWN * j, OWN), OWN)
+
+    def spread(rows):
+        return jnp.broadcast_to(b_acc[rows, :], (OWN, CH))
+
+    def exchange_cores(f):
+        for j in range(4):
+            b_s[j] = spread(block_rows(1 - core, j)).astype(BF16)
+        remote(b_s, b_c, core_send.at[3], core_recv.at[3], other_core).start()
+        for p in range(3):
+            wg_acc[p] += tap_row_grad(p, f, 1)
+            for j in range(4):
+                for q in range(3):
+                    cols = slice(128 * q, 128 * (q + 1))
+                    wg_s[p, j, q] = wg_acc[p, block_rows(1 - core, j), cols].astype(BF16)
+            remote(wg_s.at[p], wg_c.at[p], core_send.at[p], core_recv.at[p], other_core).start()
+
+    def send_share(at, j, src, dst, send_sem, recv_sem, may_stay):
+        to = 4 * core + j
+        copy = remote(src, dst, send_sem, recv_sem, {"rows": r + 2 * (at - x), "chan": to})
+        if may_stay:
+
+            @pl.when(to != c)
+            def _():
+                copy.start()
+
+            @pl.when(to == c)
+            def _():
+                local(src, dst, recv_sem).start()
+        else:
+            copy.start()
+
+    def send_shares():
         for dx in (2, 1, 3, 0):
             p = lax.rem(x + dx, xs)
 
             @pl.when(p == 3)
             def _():
-                send_shares(p, b_s, b_r, b_send, b_recv)
+                wait_bytes(b_c, core_recv.at[3])
+                for step in range(4):
+                    j = lax.rem(c + 1 + step, 4)
+                    b_t[j] = (spread(block_rows(core, j)) + b_c[j].astype(F32)).astype(BF16)
+                    send_share(p, j, b_t.at[j], b_r.at[sender], b_send, b_recv, dx == 0 and step == 3)
 
             @pl.when(p < 3)
             def _():
-                grad = (wg_acc[p] + tap_row_grad(p, f)).astype(BF16)
-                for d in range(PEERS):
+                wait_bytes(wg_c.at[p], core_recv.at[p])
+                for step in range(4):
+                    j = lax.rem(c + 1 + step, 4)
                     for q in range(3):
-                        wg_s[p, d, q] = grad[OWN * d : OWN * (d + 1), 128 * q : 128 * (q + 1)]
-                send_shares(p, wg_s.at[p], wg_r, wg_send, wg_recv)
-
-    share = 2 * far + lax.rem(r, 2)
+                        mine = wg_acc[p, block_rows(core, j), 128 * q : 128 * (q + 1)]
+                        wg_t[p, j, q] = (mine + wg_c[p, j, q].astype(F32)).astype(BF16)
+                    send_share(p, j, wg_t.at[p, j], wg_r.at[sender], wg_send, wg_recv, dx == 0 and step == 3)
 
     def send_part(src, land):
         for dfar, dx, dcore in ROW_STEPS:
@@ -401,38 +415,51 @@
             remote(src, land, part_send, part_recv, {"rows": to}).start()
         local(src, land, part_recv).start()
 
+    taps_owner = jnp.logical_and(owner, x < 3)
+    bias_owner = jnp.logical_and(owner, x == 3)
+
     def send_parts():
-        @pl.when(x < 3)
+        @pl.when(taps_owner)
         def _():
             wait_bytes(wg_r, wg_recv)
             for q in range(3):
                 acc = wg_r[0, q].astype(F32)
-                for d in range(1, xs * PEERS):
+                for d in range(1, 4 * PEERS):
                     acc += wg_r[d, q].astype(F32)
                 part[q] = acc.astype(BF16)
-            send_part(part, part_r.at[pl.ds((x * SHARES + share) * 3, 3)])
-
-        @pl.when(x == 3)
+            send_part(part, part_r.at[pl.ds((x * SHARES + far) * 3, 3)])
+
+        @pl.when(bias_owner)
         def _():
             wait_bytes(b_r, b_recv)
             acc = b_r[0].astype(F32)
-            for d in range(1, xs * PEERS):
+            for d in range(1, 4 * PEERS):
                 acc += b_r[d].astype(F32)
             part[0] = acc.astype(BF16)
-            send_part(part.at[pl.ds(0, 1)], part_r.at[pl.ds(9 * SHARES + share, 1)])
+            send_part(part.at[pl.ds(0, 1)], part_r.at[pl.ds(9 * SHARES + far, 1)])
 
     def wait_parts_sent():
-        @pl.when(x < 3)
-        def _():
-            wait_bytes(wg_r.at[pl.ds(0, 3 * PEERS - 1)], wg_send)
-            wait_bytes(b_r.at[pl.ds(0, PEERS)], b_send)
+        for p in range(3):
+            wait_bytes(wg_s.at[p], core_send.at[p])
+        wait_bytes(b_s, core_send.at[3])
+
+        @pl.when(taps_owner)
+        def _():
+            wait_bytes(wg_r.at[pl.ds(0, 11)], wg_send)
             wait_bytes(wg_r.at[pl.ds(0, ranks - 1)], part_send)
 
-        @pl.when(x == 3)
-        def _():
-            wait_bytes(wg_r.at[pl.ds(0, 3 * PEERS)], wg_send)
-            wait_bytes(b_r.at[pl.ds(0, PEERS - 1)], b_send)
+        @pl.when(jnp.logical_not(taps_owner))
+        def _():
+            wait_bytes(wg_r.at[pl.ds(0, 12)], wg_send)
+
+        @pl.when(bias_owner)
+        def _():
+            wait_bytes(b_r.at[pl.ds(0, 3)], b_send)
             wait_bytes(b_r.at[pl.ds(0, ranks - 1)], part_send)
+
+        @pl.when(jnp.logical_not(bias_owner))
+        def _():
+            wait_bytes(b_r.at[pl.ds(0, 4)], b_send)
 
     def join_phases(f):
         wait_bytes(gin_r.at[f], ret_recv.at[f])
@@ -467,25 +494,40 @@
     hear(2)
     tell(3)
     finish_pre(0)
-    make_delta(0)
+    wait_bytes(og_a.at[0], a2a_recv.at[2])
+    make_delta(0, (0, 1))
+    send_halos(delta_a, 1, 0)
     finish_pre(1)
-    add_weight_grad(0)
+    for p in range(3):
+        wg_acc[p] = tap_row_grad(p, 0, 0) + tap_row_grad(p, 0, 1)
     start_input_grad(0)
     hear(3)
-    make_delta(1)
-    send_weight_grad(1)
+    wait_bytes(og_a.at[1, pl.ds(0, 1)], a2a_recv.at[3])
+    make_delta(1, (0,))
+    for p in range(3):
+        wg_acc[p] += tap_row_grad(p, 1, 0)
+    wait_bytes(og_a.at[1, pl.ds(1, 1)], a2a_recv.at[4])
+    make_delta(1, (1,))
+    send_halos(delta_a, 1, 1)
+    exchange_cores(1)
     make_input_grad(0)
+    send_shares()
+    return_input_grad(0, 0)
+    return_input_grad(0, 1)
     start_input_grad(1)
     make_input_grad(1)
+    return_input_grad(1, 0)
     send_parts()
+    return_input_grad(1, 1)
     join_phases(0)
     join_phases(1)
     store_input_grad()
     wait_bytes(part_r, part_recv)
 
+    wait_bytes(og_s.at[0, pl.ds(0, PEERS - 1)], a2a_send.at[2])
     for f in range(2):
         wait_bytes(act_s.at[f, pl.ds(0, PEERS - 1)], a2a_send.at[f])
-        wait_bytes(og_s.at[f, pl.ds(0, PEERS - 1)], a2a_send.at[2 + f])
+        wait_bytes(og_s.at[1, pl.ds(0, PEERS - 1), pl.ds(f, 1)], a2a_send.at[3 + f])
         wait_bytes(gin_r.at[f, pl.ds(0, PEERS - 1)], ret_send.at[f])
     wait_parts_sent()
     for kind, buf in ((0, act_a), (1, delta_a)):
@@ -542,15 +584,19 @@
             vmem((16, CH, 128), F32),
             vmem((3, CH, 3 * CH), F32),
             vmem((CH, 1), F32),
-            vmem((3, PEERS, 3, OWN, CH), BF16),
+            vmem((3, 4, 3, OWN, CH), BF16),
             vmem((4 * PEERS, 3, OWN, CH), BF16),
-            vmem((PEERS, OWN, CH), BF16),
+            vmem((3, 4, 3, OWN, CH), BF16),
+            vmem((3, 4, 3, OWN, CH), BF16),
+            vmem((4, OWN, CH), BF16),
             vmem((4 * PEERS, OWN, CH), BF16),
+            vmem((4, OWN, CH), BF16),
+            vmem((4, OWN, CH), BF16),
             vmem((3, OWN, CH), BF16),
             pltpu.SemaphoreType.REGULAR((4,)),
             dma((7,)),
-            dma((4,)),
-            dma((4,)),
+            dma((5,)),
+            dma((5,)),
             dma((8,)),
             dma((8,)),
             dma((2,)),
@@ -559,6 +605,8 @@
             dma,
             dma,
             dma,
+            dma((4,)),
+            dma((4,)),
             dma,
             dma,
         ],
@@ -575,7 +623,7 @@
 
     def total(shares):
         held = [part_ref[at].astype(F32) for at in shares]
-        return (held[0] + held[1]) + (held[2] + held[3])
+        return held[0] + held[1]
 
     for p in range(3):
         for q in range(3):

time: 39.4 us -> 38.4 us (0.975)
  Pallas kernels: 38.6 us -> 37.5 us
    pallas_call x1, Pallas kernels: 37.7 us -> 36.7 us  [fused(): pl.pallas_call(functools.partial(kernel, ranks), out_shape=(vmem((OWN, he...]
where the time goes in v5:
time: 38.4 us; the launch traced here: 38.2 us
  Pallas kernels  37.5 us (98%)
  between operations  0.64 us (2%)
    pallas_call x1, Pallas kernels, fused(): pl.pallas_call(functools.partial(kernel, ranks), out_shape=(vmem((OWN, he...  36.7 us
    pallas_call x1, Pallas kernels, outputs(): pl.pallas_call(outputs_kernel, out_shape=(jax.ShapeDtypeStruct(gin.shape,...  0.84 us

profile of v5, /device:TPU:1, one launch (start us, length us, event | category | flops | bytes accessed | tf_op | source)
XLA Modules:
  0.0 38.2 jit_solution(15188860709163079552)
XLA Ops:
  0.6 36.7 %conv_backward.1 = (bf16[16,8,2048]{2,1,0:T(8,128)(2,1)S(1)}, bf16[20,16,128]{2,1,0:T(8,128)(2,1)S(1)}) custom-call(bf16[16,8,2048]{2,1,0:T(8,128)(2,1)} %bitcast.4, bf16[16,8,2048]{2,1,0:T(8,128)(2,1)} %bitcast.5, bf16[9,128,128]{2,1,0:T(8,128)(2,1)} %w_ref.1, f32[1,128]{1,0:T(1,128)} %bitcast.6), custom_call_target="tpu_custom_call" | custom-call | tf_op jit(solution)/shard_map/conv_backward/pallas_call | solution.py:550
  37.3 0.8 %conv_outputs.1 = (bf16[16,8,2048]{2,1,0:T(8,128)(2,1)}, f32[9,16,128]{2,1,0:T(8,128)}, f32[16]{0:T(128)}) custom-call(bf16[16,8,2048]{2,1,0:T(8,128)(2,1)S(1)} %get-tuple-element.8.gin_ref, bf16[20,16,128]{2,1,0:T(8,128)(2,1)S(1)} %get-tuple-element.9.part_ref), custom_call_target="tpu_custom_call" | custom-call | tf_op jit(solution)/shard_map/conv_outputs/pallas_call | solution.py:646
